TPU v7x, 32 devices: a whole 2x2x4 slice. The times are simulated.
32 devices in a mesh: dp: 4 (over y, core), expert: 8 (over z, x).
Axes of the slice: x: 2, y: 2, z: 4, core: 2. Of those that a mesh axis runs over, the one named last changes fastest.
Arguments:
- tokens: bfloat16 [4096, 2048], P(('dp', 'expert')), may hold values from -6 to 6
- out_grad: bfloat16 [4096, 2048], P(('dp', 'expert')), may hold values from -6 to 6
- expert_ids: int32 [4096, 8], P(('dp', 'expert')), may hold values from 0 to 127, all different within a row; in each aligned block of 128 rows (0 to 127, 128 to 255, ...) at most 10 rows name the same one
- gates: bfloat16 [4096, 8], P(('dp', 'expert')), may hold values from 0.049804688 to 0.59765625
- expert_weights: bfloat16 [8, 3, 2048, 384], P('expert', None, 'dp'), may hold values from -0.125 to 0.125
Outputs:
- token_grads: bfloat16 [4096, 2048], P(('dp', 'expert'))
- weight_grads: float32 [8, 3, 2048, 384], P('expert', None, 'dp')
Inputs may be any that keep to these rules, and one draw needn't show every extreme that they name: `expert_ids`: each row names 8 different experts; among the 128 rows of one device no expert is named more than 10 times, a bound that some block reaches.
All inputs are finite; a program needn't handle non-finite values.
Results may differ from a plain program's by a relative error of at most 0.0065.
Values may be sent and summed in bfloat16 or wider, within the bound.
No kernel may reach another device: no remote copies, remote signals or barrier semaphores. Data moves between devices by JAX's collectives and lax.ppermute only.
A program may use at most 64 MiB of HBM per device.

v0:
```python
import jax
import jax.numpy as jnp
from jax import lax
from jax.experimental import pallas as pl
from jax.experimental.pallas import tpu as pltpu
from jax.sharding import PartitionSpec as P

SLOTS = 10
WIDE = 512
JOIN = 4
F32 = jnp.float32
BF16 = jnp.bfloat16


def dot(first_op, second_op):
    return jnp.dot(first_op, second_op, preferred_element_type=F32)


def dot_tn(first_op, second_op):
    return lax.dot_general(first_op, second_op, (((0,), (0,)), ((), ())), preferred_element_type=F32)


def dot_nt(first_op, second_op):
    return lax.dot_general(first_op, second_op, (((1,), (1,)), ((), ())), preferred_element_type=F32)


def swap(value, bits):
    return lax.ppermute(value, "dp", [(i, i ^ bits) for i in range(lax.axis_size("dp"))])


def piece_rows(chunks):
    return -(-chunks * SLOTS // 8) * 8


def params(*arrays):
    moved = sum(a.size * a.dtype.itemsize for a in arrays)
    return pltpu.CompilerParams(vmem_limit_bytes=min(56 * 2**20, 6 * 2**20 + 3 * moved // 2))


def cost(flops, moved):
    return pl.CostEstimate(flops=flops, bytes_accessed=moved, transcendentals=0)


def shape(*extent, kind=BF16):
    return jax.ShapeDtypeStruct(extent, kind)


def lower(value, by):
    return jnp.floor((value + 0.5) * (1.0 / by))


def sort_matrix(parts, chunks, transposed):
    padded = piece_rows(chunks)
    wide, tall = JOIN * parts * padded, parts * chunks * JOIN * SLOTS
    extent, axis = ((wide, tall), 0) if transposed else ((tall, wide), 1)
    line = (wide, 1) if transposed else (1, wide)
    place = lax.broadcasted_iota(jnp.int32, line, axis).astype(F32)
    block = lower(place, padded)
    inside = place - block * padded
    source = lower(block, parts)
    part = block - source * parts
    chunk = lower(inside, SLOTS)
    slot = inside - chunk * SLOTS
    target = ((part * chunks + chunk) * JOIN + source) * SLOTS + slot
    target = jnp.where(chunk < chunks, target, -1.0)
    spots = lax.broadcasted_iota(jnp.int32, extent, 1 - axis).astype(F32)
    return jnp.where(spots == target, 1.0, 0.0).astype(BF16)


def table_of(code, values, chunks, padded):
    window, token_rows = code.shape
    spots = lax.broadcasted_iota(jnp.int32, (padded, chunks * token_rows), 0).astype(F32)
    tables = []
    for expert in range(window):
        own = code[expert : expert + 1]
        hit = spots == jnp.concatenate([own + float(SLOTS * c) for c in range(chunks)], axis=1)
        row = []
        for value in values:
            if value is None:
                row.append(jnp.where(hit, 1.0, 0.0))
            else:
                gate = jnp.concatenate([value[expert : expert + 1]] * chunks, axis=1)
                row.append(jnp.where(hit, gate, 0.0))
        tables.append(row)
    return [jnp.concatenate([t[i] for t in tables], axis=0) for i in range(len(values))]


def token_kernel(token_ref):
    token_ref[...] = jnp.zeros_like(token_ref)


def pack_kernel(ids_ref, gates_ref, tokens_ref, grads_ref, _, sent_ref, code_ref):
    token_rows, model_width = tokens_ref.shape
    window = code_ref.shape[0]
    chunks = model_width // WIDE
    padded = piece_rows(chunks)
    above = lax.broadcasted_iota(jnp.int32, (token_rows, token_rows), 0)
    along = lax.broadcasted_iota(jnp.int32, (token_rows, token_rows), 1)
    earlier = jnp.where(above < along, 1.0, 0.0).astype(BF16)
    ids = ids_ref[...]
    gates = gates_ref[...].astype(F32)
    members, chosen = [], []
    for expert in range(window):
        hit = ids == expert
        members.append(jnp.sum(jnp.where(hit, 1.0, 0.0), axis=0, keepdims=True))
        chosen.append(jnp.sum(jnp.where(hit, gates, 0.0), axis=0, keepdims=True))
    members = jnp.concatenate(members, axis=0)
    chosen = jnp.concatenate(chosen, axis=0)
    code = jnp.where(members > 0.0, dot(members.astype(BF16), earlier), -1e6)
    code_ref[...] = code
    table, gated = table_of(code, [None, chosen], chunks, padded)

    def columns(ref):
        return jnp.concatenate([ref[:, c * WIDE : (c + 1) * WIDE] for c in range(chunks)], axis=0)

    rows = dot(table.astype(BF16), columns(tokens_ref))
    grads = dot(gated.astype(BF16), columns(grads_ref))
    for expert in range(window):
        lines = slice(expert * padded, (expert + 1) * padded)
        sent_ref[expert] = jnp.concatenate([rows[lines], grads[lines]], axis=0).astype(BF16)


def table_kernel(chunks, code_ref, table_ref):
    (table,) = table_of(code_ref[...], [None], chunks, piece_rows(chunks))
    table_ref[...] = table.T.astype(BF16)


def part_kernel(acts_ref, *refs):
    hidden_units = acts_ref.shape[1] // 3
    for at, ref in enumerate(refs[-3:]):
        ref[...] = acts_ref[:, at * hidden_units : (at + 1) * hidden_units]


def keep_kernel(*refs):
    pass


def place(source, pair_ref, down_ref, sems, at):
    hidden_units = down_ref.shape[1]
    moves = [
        (source.at[0], pair_ref.at[:, pl.ds(0, hidden_units)]),
        (source.at[1], pair_ref.at[:, pl.ds(hidden_units, hidden_units)]),
        (source.at[2], down_ref),
    ]
    return [
        pltpu.make_async_copy(start, end, sems.at[at, which]) for which, (start, end) in enumerate(moves)
    ]


def partial_kernel(groups, got_ref, own_in, near_in, *refs):
    (out_ref, rows_ref, grads_ref, pair_ref, token_ref), refs = refs[:5], refs[5:]
    slices_refs, (down_ref, sems) = refs[: groups - 1], refs[groups - 1 :]
    copies = [
        copy
        for b, source in enumerate((own_in.at[0], near_in.at[0]))
        for copy in place(source, pair_ref.at[b], down_ref.at[b], sems, b)
    ]
    for copy in copies:
        copy.start()
    token_ref[...] = jnp.zeros_like(token_ref)
    sources, height, _ = got_ref.shape
    model_width = rows_ref.shape[1]
    chunks = model_width // WIDE
    owned = model_width // groups
    joined = sources // JOIN
    tall = JOIN * SLOTS
    blocks = jnp.concatenate(
        [got_ref[q * JOIN : (q + 1) * JOIN].reshape(JOIN * height, WIDE) for q in range(joined)],
        axis=1,
    )
    lines = dot(sort_matrix(2, chunks, False), blocks)

    def gathered(part):
        return jnp.concatenate(
            [
                jnp.concatenate(
                    [
                        lines[
                            (part * chunks + c) * tall : (part * chunks + c + 1) * tall,
                            q * WIDE : (q + 1) * WIDE,
                        ]
                        for c in range(chunks)
                    ],
                    axis=1,
                )
                for q in range(joined)
            ],
            axis=0,
        ).astype(BF16)

    rows_ref[...] = gathered(0)
    grads_ref[...] = gathered(1)
    me = lax.axis_index("dp")
    wide = pair_ref.shape[2]
    for copy in copies:
        copy.wait()
    pair_sum, down_sum = None, None
    for b in range(groups):
        lanes = pl.ds(pl.multiple_of((me ^ b) * owned, 128), owned)
        rows, grads = rows_ref[:, lanes], grads_ref[:, lanes]
        target, first = (slices_refs[0], 2) if b == 0 else (slices_refs[b - 1], 0)
        target[first] = rows
        target[first + 1] = grads
        if b < 2:
            term = dot(rows, pair_ref[b])
            pair_sum = term if pair_sum is None else pair_sum + term
            term = dot(grads, down_ref[b])
            down_sum = term if down_sum is None else down_sum + term
    out_ref[:, :wide] = pair_sum
    out_ref[:, wide:] = down_sum


def lanes_of(owner, owned):
    return pl.ds(pl.multiple_of(owner * owned, 128), owned)


def far_kernel(groups, rows_ref, grads_ref, partial_ref, *refs):
    far = range(2, groups, 2)
    weights_in, (out_ref, pair_ref, down_ref, sems) = refs[: len(far)], refs[len(far) :]
    copies = [
        place(source.at[0], pair_ref.at[at], down_ref.at[at], sems, at)
        for at, source in enumerate(weights_in)
    ]
    for some in copies:
        for copy in some:
            copy.start()
    me = lax.axis_index("dp")
    owned, wide = pair_ref.shape[1:]
    pair_sum, down_sum = partial_ref[:, :wide], partial_ref[:, wide:]
    for at, b in enumerate(far):
        for copy in copies[at]:
            copy.wait()
        lanes = lanes_of(me ^ b, owned)
        pair_sum = pair_sum + dot(rows_ref[:, lanes], pair_ref[at])
        down_sum = down_sum + dot(grads_ref[:, lanes], down_ref[at])
    out_ref[:, :wide] = pair_sum
    out_ref[:, wide:] = down_sum


def back_kernel(groups, rows_ref, grads_ref, partial_ref, near_ref, far_ref, *refs):
    last_refs, (acts_ref, out_ref, back_ref) = refs[:-3], refs[-3:]
    me = lax.axis_index("dp")
    model_width = grads_ref.shape[1]
    owned = model_width // groups
    chunks = model_width // WIDE
    hidden_units = partial_ref.shape[1] // 3
    wide = 2 * hidden_units

    def lanes(b):
        return lanes_of(me ^ b, owned)

    gate_act = partial_ref[:, :hidden_units]
    up_act = partial_ref[:, hidden_units:wide]
    grad_hidden = partial_ref[:, wide:]
    for at, ref in enumerate(last_refs):
        here = lanes(2 * at + 3)
        gate_act = gate_act + dot(rows_ref[:, here], ref[0, 0])
        up_act = up_act + dot(rows_ref[:, here], ref[0, 1])
        grad_hidden = grad_hidden + dot(grads_ref[:, here], ref[0, 2])
    logistic = jax.nn.sigmoid(gate_act)
    swish_out = gate_act * logistic
    hidden = (swish_out * up_act).astype(BF16)
    grad_up = (grad_hidden * swish_out).astype(BF16)
    grad_gate = (grad_hidden * up_act * logistic * (1.0 + gate_act * (1.0 - logistic))).astype(BF16)
    acts = jnp.concatenate([grad_gate, grad_up], axis=1)
    acts_ref[:, :wide] = acts
    acts_ref[:, wide:] = hidden
    for b in range(groups):
        if b < 2:
            term = dot_nt(acts, near_ref[b])
        elif b % 2 == 0:
            term = dot_nt(acts, far_ref[b // 2 - 1])
        else:
            ref = last_refs[b // 2 - 1]
            term = dot_nt(grad_gate, ref[0, 0]) + dot_nt(grad_up, ref[0, 1])
        back_ref[:, lanes(b)] = term
    tall = JOIN * SLOTS
    joined = grads_ref.shape[0] // tall
    lines = jnp.concatenate(
        [
            jnp.concatenate(
                [
                    back_ref[q * tall : (q + 1) * tall, c * WIDE : (c + 1) * WIDE]
                    for c in range(chunks)
                ],
                axis=0,
            )
            for q in range(joined)
        ],
        axis=1,
    ).astype(BF16)
    blocks = dot(sort_matrix(1, chunks, True), lines)
    height = piece_rows(chunks)
    for q in range(joined):
        for j in range(JOIN):
            part = blocks[j * height : (j + 1) * height, q * WIDE : (q + 1) * WIDE]
            out_ref[q * JOIN + j] = part.astype(BF16)


def combine_kernel(returned_ref, table_ref, out_ref, held_ref, sems):
    token_rows, model_width = held_ref.shape
    window, height, _ = returned_ref.shape
    lines = returned_ref[...].astype(F32).reshape(window * height, WIDE).astype(BF16)
    parts = sems.shape[0]
    chunks = model_width // WIDE // parts
    copies = []
    for part in range(parts):
        table = table_ref[part * chunks * token_rows : (part + 1) * chunks * token_rows]
        result = dot(table, lines).astype(BF16)
        for c in range(chunks):
            at = part * chunks + c
            held_ref[:, at * WIDE : (at + 1) * WIDE] = result[c * token_rows : (c + 1) * token_rows]
        lanes = pl.ds(part * chunks * WIDE, chunks * WIDE)
        copies.append(
            pltpu.make_async_copy(held_ref.at[:, lanes], out_ref.at[:, lanes], sems.at[part])
        )
        copies[-1].start()
    for copy in copies:
        copy.wait()


def grads_kernel(groups, *refs):
    slices_refs, acts_refs, (out_ref, held_ref, sems) = refs[:groups], refs[groups:-3], refs[-3:]
    hidden_units = out_ref.shape[3]
    copies = [pltpu.make_async_copy(held_ref.at[at], out_ref.at[0, at], sems.at[at]) for at in range(3)]
    rows_here = acts_refs[0].shape[0]
    step = max(1, min(groups, 640 // rows_here))
    for at in range(3):
        lanes = slice(at * hidden_units, (at + 1) * hidden_units)
        kind = 0 if at < 2 else 1
        places = [kind + 2 if b == 0 else kind for b in range(groups)]
        total = None
        for first in range(0, groups, step):
            some = range(first, first + step)
            rows = jnp.concatenate([slices_refs[b][places[b]] for b in some], axis=0)
            acts = jnp.concatenate(
                [
                    acts_refs[b][:, lanes] if b < 2 else acts_refs[2 + 3 * (b - 2) + at][...]
                    for b in some
                ],
                axis=0,
            )
            term = dot_tn(rows, acts)
            total = term if total is None else total + term
        held_ref[at] = total
        copies[at].start()
    for copy in copies:
        copy.wait()


def on_device(tokens, out_grad, expert_ids, gates, expert_weights):
    window = lax.axis_size("expert")
    groups = lax.axis_size("dp")
    token_rows, model_width = tokens.shape
    hidden_units = expert_weights.shape[3]
    owned = model_width // groups
    chunks = model_width // WIDE
    padded = piece_rows(chunks)
    rows_here = window * SLOTS
    wide = 2 * hidden_units
    anywhere = pl.BlockSpec(memory_space=pl.ANY)

    far = list(range(2, groups, 2))
    token = pl.pallas_call(
        token_kernel,
        out_shape=shape(8, 128, kind=F32),
        compiler_params=params(),
        cost_estimate=cost(10**11, 10**8),
    )()
    arriving = [swap(expert_weights, b) for b in far]
    near = swap(expert_weights, 1)

    ids_t, gates_t = expert_ids.T, gates.T
    sent, code = pl.pallas_call(
        pack_kernel,
        out_shape=(
            shape(window, 2 * padded, WIDE),
            shape(window, token_rows, kind=F32),
        ),
        compiler_params=params(tokens, out_grad),
    )(ids_t, gates_t, tokens, out_grad, token)

    got = lax.all_to_all(sent, "expert", split_axis=0, concat_axis=0, tiled=True)
    table = pl.pallas_call(
        lambda *refs: table_kernel(chunks, *refs),
        out_shape=shape(chunks * token_rows, window * padded),
        compiler_params=params(),
        cost_estimate=cost(10**6, 10**5),
    )(code)

    outs = pl.pallas_call(
        lambda *refs: partial_kernel(groups, *refs),
        in_specs=[pl.BlockSpec()] + [anywhere] * 2,
        out_shape=[
            shape(rows_here, 3 * hidden_units, kind=F32),
            shape(rows_here, model_width),
            shape(rows_here, model_width),
            shape(2, owned, wide),
            shape(8, 128, kind=F32),
        ]
        + [shape(4, rows_here, owned)]
        + [shape(2, rows_here, owned)] * (groups - 2),
        scratch_shapes=[
            pltpu.VMEM((2, owned, hidden_units), BF16),
            pltpu.SemaphoreType.DMA((2, 3)),
        ],
        compiler_params=params(got, expert_weights, expert_weights),
    )(got, expert_weights, near)
    partial, rows, grads, near_pairs, token = outs[:5]
    slices = list(outs[5:])
    slices = slices[:1] + [swap(slices[b - 1], b) for b in range(1, groups)]

    arrived = pl.pallas_call(
        keep_kernel,
        in_specs=[anywhere] * (len(far) + 1),
        out_specs=[anywhere] * len(far),
        out_shape=[shape(*expert_weights.shape)] * len(far),
        input_output_aliases={at + 1: at for at in range(len(far))},
        compiler_params=params(),
        cost_estimate=cost(10**11, 10**8),
    )(token, *arriving)
    last = [swap(value, 1) for value in arrived]
    partial, far_pairs = pl.pallas_call(
        lambda *refs: far_kernel(groups, *refs),
        in_specs=[pl.BlockSpec()] * 3 + [anywhere] * len(far),
        out_shape=(shape(rows_here, 3 * hidden_units, kind=F32), shape(len(far), owned, wide)),
        scratch_shapes=[
            pltpu.VMEM((len(far), owned, hidden_units), BF16),
            pltpu.SemaphoreType.DMA((len(far), 3)),
        ],
        compiler_params=params(rows, grads, *arrived, *arrived),
    )(rows, grads, partial, *arrived)

    acts, back = pl.pallas_call(
        lambda *refs: back_kernel(groups, *refs),
        out_shape=(shape(rows_here, 3 * hidden_units), shape(window, padded, WIDE)),
        scratch_shapes=[pltpu.VMEM((rows_here, model_width), F32)],
        compiler_params=params(rows, grads, partial, near_pairs, far_pairs, *last),
        cost_estimate=cost(10**6, 10**5),
    )(rows, grads, partial, near_pairs, far_pairs, *last)
    returned = lax.all_to_all(back, "expert", split_axis=0, concat_axis=0, tiled=True)

    later = pl.pallas_call(
        token_kernel,
        out_shape=shape(16, 128, kind=F32),
        compiler_params=params(),
        cost_estimate=cost(10**11, 10**8),
    )()
    parts = pl.pallas_call(
        part_kernel,
        in_specs=[pl.BlockSpec()] + [anywhere] * groups,
        out_shape=[shape(rows_here, hidden_units)] * 3,
        compiler_params=params(acts, acts),
        cost_estimate=cost(10**6, 10**5),
    )(acts, later, *slices[1:])
    every = slices + [acts, swap(acts, 1)]
    for b in far:
        over = [swap(part, b) for part in parts]
        every += over + [swap(part, 1) for part in over]
    weight_grads = pl.pallas_call(
        lambda *refs: grads_kernel(groups, *refs),
        out_specs=anywhere,
        out_shape=shape(1, 3, owned, hidden_units, kind=F32),
        scratch_shapes=[
            pltpu.VMEM((3, owned, hidden_units), F32),
            pltpu.SemaphoreType.DMA((3,)),
        ],
        compiler_params=params(*every, expert_weights, expert_weights),
        cost_estimate=cost(6 * groups * rows_here * owned * hidden_units, 12 * owned * hidden_units),
    )(*every)

    token_grads = pl.pallas_call(
        combine_kernel,
        out_specs=anywhere,
        out_shape=shape(token_rows, model_width),
        scratch_shapes=[pltpu.VMEM((token_rows, model_width), BF16), pltpu.SemaphoreType.DMA((2,))],
        compiler_params=params(table, back, tokens),
    )(returned, table)
    return (token_grads, weight_grads)


def solution(mesh):
    lines = P(("dp", "expert"), None)
    slabs = P("expert", None, "dp", None)
    return jax.shard_map(
        on_device,
        mesh=mesh,
        in_specs=(lines, lines, lines, lines, slabs),
        out_specs=(lines, slabs),
        check_vma=False,
    )
```

profile of v0, /device:TPU:0, one launch (start us, length us, event | category | flops | bytes accessed | tf_op | source)
XLA Modules:
  0.0 53.9 jit_solution(12969602419957275456)
XLA Ops:
  0.7 0.5 collective-permute-start
  1.2 2.6 %collective-permute-start.1 = (bf16[1,3,512,384]{3,2,1,0:T(8,128)(2,1)}, bf16[1,3,512,384]{3,2,1,0:T(8,128)(2,1)S(1)}, u32[]{:S(2)}, u32[]{:S(2)}) collective-permute-start(bf16[1,3,512,384]{3,2,1,0:T(8,128)(2,1)} %refs_1_.1), channel_id=1, source_target_pairs={{0,16},{8,24},{16,0},{24,8},{1,17},{9,25},{17,1},{25,9},{2,18},{10... | collective-permute-start | bytes 3538952 | tf_op jit(solution)/shard_map/ppermute | solution.py:28
  3.8 0.0 copy-start
  3.8 0.6 %shard_map.69 = (bf16[8,80,512]{2,1,0:T(8,128)(2,1)S(1)}, f32[8,128]{1,0:T(8,128)S(1)}) custom-call(s32[8,128]{1,0:T(8,128)S(1)} %bitcast.2, bf16[8,128]{1,0:T(8,128)(2,1)S(1)} %bitcast.3, bf16[128,2048]{1,0:T(8,128)(2,1)S(1)} %copy-done.1, bf16[128,2048]{1,0:T(8,128)(2,1)S(1)} %copy-done.2, f32[8,128]{1,0:T(8,128)S(1)} %shard_map.68._), custom_call_target="tpu_custom_call" | custom-call | tf_op jit(solution)/shard_map/pallas_call | solution.py:374
  4.5 23.6 %all_to_all.10.refs_0_ = bf16[8,80,512]{2,1,0:T(8,128)(2,1)S(1)} all-to-all(bf16[8,80,512]{2,1,0:T(8,128)(2,1)S(1)} %get-tuple-element.19), channel_id=1, replica_groups=mesh['dp'=4,'expert'=8] {'expert'}, dimensions={0} | all-to-all | bytes 1310720 | tf_op jit(solution)/shard_map/all_to_all | solution.py:383
  28.1 0.0 collective-permute-done.refs_2_
  28.1 1.7 %shard_map.70 = (f32[80,1152]{1,0:T(8,128)S(1)}, bf16[80,2048]{1,0:T(8,128)(2,1)S(1)}, bf16[80,2048]{1,0:T(8,128)(2,1)S(1)}, bf16[2,512,768]{2,1,0:T(8,128)(2,1)...) custom-call(bf16[8,80,512]{2,1,0:T(8,128)(2,1)S(1)} %all_to_all.10.r, ...), custom_call_target="tpu_custom_call" | custom-call | tf_op jit(solution)/shard_map/pallas_call | solution.py:391
  29.7 0.8 %collective-permute-done.1.refs_1_ = bf16[1,3,512,384]{3,2,1,0:T(8,128)(2,1)S(1)} collective-permute-done((bf16[1,3,512,384]{3,2,1,0:T(8,128)(2,1)}, bf16[1,3,512,384]{3,2,1,0:T(8,128)(2,1)S(1)}, u32[]{:S(2)}, u32[]{:S(2)}) %collective-permute-start.1) | collective-permute-done | bytes 1179680 | tf_op jit(solution)/shard_map/ppermute | solution.py:28
  30.6 0.0 collective-permute-start.2
  30.6 0.5 collective-permute-start.3
  31.1 1.8 %collective-permute-start.4 = (bf16[2,80,512]{2,1,0:T(8,128)(2,1)S(1)}, bf16[2,80,512]{2,1,0:T(8,128)(2,1)S(1)}, u32[]{:S(2)}, u32[]{:S(2)}) collective-permute-start(bf16[2,80,512]{2,1,0:T(8,128)(2,1)S(1)} %get-tuple-element.30), channel_id=1, source_target_pairs={{0,16},{8,24},{16,0},{24,8},{1,17},{9,25},{17,1},{25,9},{2,18},{10... | collective-permute-start | bytes 491528 | tf_op jit(solution)/shard_map/ppermute | solution.py:28
  32.8 0.0 collective-permute-start.5
  32.8 0.7 %shard_map.72 = (f32[80,1152]{1,0:T(8,128)S(1)}, bf16[1,512,768]{2,1,0:T(8,128)(2,1)S(1)}) custom-call(bf16[80,2048]{1,0:T(8,128)(2,1)S(1)} %get-tuple-element.20.refs_0_, bf16[80,2048]{1,0:T(8,128)(2,1)S(1)} %get-tuple-element.21.refs_1_, f32[80,1152]{1,0:T(8,128)S(1)} %get-tuple-element.22.refs_2_, bf16[1,3,512,384]{3,2,1,0:T(8,128)(2,1)S(1)} %shard_map.71.refs_3_), custom_call_target="tpu_custom_call" | custom-call | tf_op jit(solution)/shard_map/pallas_call | solution.py:423
  33.5 0.0 collective-permute-done.2.refs_5_
  33.5 2.3 %shard_map.73 = (bf16[80,1152]{1,0:T(8,128)(2,1)S(1)}, bf16[8,40,512]{2,1,0:T(8,128)(2,1)}) custom-call(bf16[80,2048]{1,0:T(8,128)(2,1)S(1)} %get-tuple-element.20.refs_0_, bf16[80,2048]{1,0:T(8,128)(2,1)S(1)} %get-tuple-element.21.refs_1_, f32[80,1152]{1,0:T(8,128)S(1)} %get-tuple-element.24.refs_2_, bf16[2,512,768]{2,1,0:T(8,128)(2,1)S(1)} %get-tuple-element.25.refs_3_, ...), custom_call_target="tpu_custom_call" | custom-call | flops 1000000 | bytes 100000 | tf_op jit(solution)/shard_map/pallas_call | solution.py:434
  35.8 0.4 collective-permute-start.6
  36.2 6.0 %all-to-all-start.1 = ((bf16[8,40,512]{2,1,0:T(8,128)(2,1)}), bf16[8,40,512]{2,1,0:T(8,128)(2,1)S(1)}, u32[]{:S(2)}, u32[]{:S(2)}) async-start(bf16[8,40,512]{2,1,0:T(8,128)(2,1)} %get-tuple-element.27), calls=%async_computation.1 | async-start | bytes 655360 | tf_op jit(solution)/shard_map/all_to_all | solution.py:441
  42.2 0.0 collective-permute-done.4.refs_2_
  42.2 0.0 collective-permute-done.5.refs_3_
  42.3 1.6 %collective-permute-start.7 = (bf16[80,384]{1,0:T(8,128)(2,1)S(1)}, bf16[80,384]{1,0:T(8,128)(2,1)S(1)}, u32[]{:S(2)}, u32[]{:S(2)}) collective-permute-start(bf16[80,384]{1,0:T(8,128)(2,1)S(1)} %get-tuple-element.33), channel_id=1, source_target_pairs={{0,16},{8,24},{16,0},{24,8},{1,17},{9,25},{17,1},{25,9},{2,18},{10... | collective-permute-start | bytes 184328 | tf_op jit(solution)/shard_map/ppermute | solution.py:28
  43.9 0.5 collective-permute-start.8
  44.4 1.5 %collective-permute-start.9 = (bf16[80,384]{1,0:T(8,128)(2,1)S(1)}, bf16[80,384]{1,0:T(8,128)(2,1)S(1)}, u32[]{:S(2)}, u32[]{:S(2)}) collective-permute-start(bf16[80,384]{1,0:T(8,128)(2,1)S(1)} %get-tuple-element.35), channel_id=1, source_target_pairs={{0,16},{8,24},{16,0},{24,8},{1,17},{9,25},{17,1},{25,9},{2,18},{10... | collective-permute-start | bytes 184328 | tf_op jit(solution)/shard_map/ppermute | solution.py:28
  45.9 1.3 %collective-permute-done.7.refs_6_ = bf16[80,384]{1,0:T(8,128)(2,1)S(1)} collective-permute-done((bf16[80,384]{1,0:T(8,128)(2,1)S(1)}, bf16[80,384]{1,0:T(8,128)(2,1)S(1)}, u32[]{:S(2)}, u32[]{:S(2)}) %collective-permute-start.7) | collective-permute-done | bytes 61472 | tf_op jit(solution)/shard_map/ppermute | solution.py:28
  47.2 1.3 %collective-permute-done.8.refs_7_ = bf16[80,384]{1,0:T(8,128)(2,1)S(1)} collective-permute-done((bf16[80,384]{1,0:T(8,128)(2,1)S(1)}, bf16[80,384]{1,0:T(8,128)(2,1)S(1)}, u32[]{:S(2)}, u32[]{:S(2)}) %collective-permute-start.8) | collective-permute-done | bytes 61472 | tf_op jit(solution)/shard_map/ppermute | solution.py:28
  48.6 0.0 collective-permute-start.11
  48.6 0.7 %collective-permute-done.9.refs_8_ = bf16[80,384]{1,0:T(8,128)(2,1)S(1)} collective-permute-done((bf16[80,384]{1,0:T(8,128)(2,1)S(1)}, bf16[80,384]{1,0:T(8,128)(2,1)S(1)}, u32[]{:S(2)}, u32[]{:S(2)}) %collective-permute-start.9) | collective-permute-done | bytes 61472 | tf_op jit(solution)/shard_map/ppermute | solution.py:28
  49.2 0.2 shard_map.74.table_ref
  49.4 0.4 collective-permute-done.11.refs_10_
  49.8 0.7 %collective-permute-done.12.refs_11_ = bf16[80,384]{1,0:T(8,128)(2,1)S(1)} collective-permute-done((bf16[80,384]{1,0:T(8,128)(2,1)S(1)}, bf16[80,384]{1,0:T(8,128)(2,1)S(1)}, u32[]{:S(2)}, u32[]{:S(2)}) %collective-permute-start.12) | collective-permute-done | bytes 61472 | tf_op jit(solution)/shard_map/ppermute | solution.py:28
  50.5 1.9 %shard_map.78 = f32[1,3,512,384]{3,2,1,0:T(8,128)} custom-call(bf16[4,80,512]{2,1,0:T(8,128)(2,1)S(1)} %get-tuple-element.29.refs_0_, bf16[4,80,512]{2,1,0:T(8,128)(2,1)S(1)} %collective-permute-done.3.refs_1_, bf16[2,80,512]{2,1,0:T(8,128)(2,1)S(1)} %collective-permute-done.4.refs_2_, bf16[2,80,512]{2,1,0:T(8,128)(2,1)S(1)} %collective-permute-done.5.refs_3_, ...), custom_call_target="tpu_custom_call" | custom-call | flops 377487360 | bytes 2359296 | tf_op jit(solution)/shard_map/pallas_call | solution.py:460
  52.4 0.3 all-to-all-done.1.returned_ref
  52.7 1.2 %shard_map.75 = bf16[128,2048]{1,0:T(8,128)(2,1)} custom-call(bf16[8,40,512]{2,1,0:T(8,128)(2,1)S(1)} %all-to-all-done.1.returned_ref, bf16[512,320]{1,0:T(8,128)(2,1)S(1)} %shard_map.74.table_ref), custom_call_target="tpu_custom_call" | custom-call | tf_op jit(solution)/shard_map/pallas_call | solution.py:472
  (18 shorter events, 0.1 us)
Async XLA Ops:
  0.6 3.2 %copy-start.3 = (s32[128,8]{0,1:T(8,128)S(1)}, s32[128,8]{0,1:T(8,128)}, u32[]{:S(2)}) copy-start(s32[128,8]{0,1:T(8,128)} %param.7) | copy-start | bytes 12292
  0.6 3.2 %copy-start.4 = (bf16[128,8]{0,1:T(8,128)(2,1)S(1)}, bf16[128,8]{0,1:T(8,128)(2,1)}, u32[]{:S(2)}) copy-start(bf16[128,8]{0,1:T(8,128)(2,1)} %param.8) | copy-start | bytes 6148
  0.7 3.1 %copy-start.1 = (bf16[128,2048]{1,0:T(8,128)(2,1)S(1)}, bf16[128,2048]{1,0:T(8,128)(2,1)}, u32[]{:S(2)}) copy-start(bf16[128,2048]{1,0:T(8,128)(2,1)} %tokens_ref.1) | copy-start | bytes 1572868
  0.7 3.1 %copy-start.2 = (bf16[128,2048]{1,0:T(8,128)(2,1)S(1)}, bf16[128,2048]{1,0:T(8,128)(2,1)}, u32[]{:S(2)}) copy-start(bf16[128,2048]{1,0:T(8,128)(2,1)} %grads_ref.1) | copy-start | bytes 1572868
  0.7 27.4 %collective-permute-start = (bf16[1,3,512,384]{3,2,1,0:T(8,128)(2,1)}, bf16[1,3,512,384]{3,2,1,0:T(8,128)(2,1)S(1)}, u32[]{:S(2)}, u32[]{:S(2)}) collective-permute-start(bf16[1,3,512,384]{3,2,1,0:T(8,128)(2,1)} %refs_1_.1), channel_id=1, source_target_pairs={{0,8},{8,0},{16,24},{24,16},{1,9},{9,1},{17,25},{25,17},{2,10},{10... | collective-permute-start | bytes 3538952 | tf_op jit(solution)/shard_map/ppermute | solution.py:28
  1.2 29.4 %collective-permute-start.1 = (bf16[1,3,512,384]{3,2,1,0:T(8,128)(2,1)}, bf16[1,3,512,384]{3,2,1,0:T(8,128)(2,1)S(1)}, u32[]{:S(2)}, u32[]{:S(2)}) collective-permute-start(bf16[1,3,512,384]{3,2,1,0:T(8,128)(2,1)} %refs_1_.1), channel_id=1, source_target_pairs={{0,16},{8,24},{16,0},{24,8},{1,17},{9,25},{17,1},{25,9},{2,18},{10... | collective-permute-start | bytes 3538952 | tf_op jit(solution)/shard_map/ppermute | solution.py:28
  3.8 24.3 %copy-start = (bf16[1,3,512,384]{3,2,1,0:T(8,128)(2,1)S(1)}, bf16[1,3,512,384]{3,2,1,0:T(8,128)(2,1)}, u32[]{:S(2)}) copy-start(bf16[1,3,512,384]{3,2,1,0:T(8,128)(2,1)} %refs_1_.1) | copy-start | bytes 3538948
  30.6 2.9 %collective-permute-start.2 = (bf16[1,3,512,384]{3,2,1,0:T(8,128)(2,1)S(1)}, bf16[1,3,512,384]{3,2,1,0:T(8,128)(2,1)S(1)}, u32[]{:S(2)}, u32[]{:S(2)}) collective-permute-start(bf16[1,3,512,384]{3,2,1,0:T(8,128)(2,1)S(1)} %shard_map.71.refs_3_), channel_id=1, source_target_pairs={{0,8},{8,0},{16,24},{24,16},{1,9},{9,1},{17,25},{25,17},{2,10},{10... | collective-permute-start | bytes 3538952 | tf_op jit(solution)/shard_map/ppermute | solution.py:28
  30.6 11.7 %collective-permute-start.3 = (bf16[4,80,512]{2,1,0:T(8,128)(2,1)S(1)}, bf16[4,80,512]{2,1,0:T(8,128)(2,1)S(1)}, u32[]{:S(2)}, u32[]{:S(2)}) collective-permute-start(bf16[4,80,512]{2,1,0:T(8,128)(2,1)S(1)} %get-tuple-element.29.refs_0_), channel_id=1, source_target_pairs={{0,8},{8,0},{16,24},{24,16},{1,9},{9,1},{17,25},{25,17},{2,10},{10... | collective-permute-start | bytes 983048 | tf_op jit(solution)/shard_map/ppermute | solution.py:28
  31.1 11.2 %collective-permute-start.4 = (bf16[2,80,512]{2,1,0:T(8,128)(2,1)S(1)}, bf16[2,80,512]{2,1,0:T(8,128)(2,1)S(1)}, u32[]{:S(2)}, u32[]{:S(2)}) collective-permute-start(bf16[2,80,512]{2,1,0:T(8,128)(2,1)S(1)} %get-tuple-element.30), channel_id=1, source_target_pairs={{0,16},{8,24},{16,0},{24,8},{1,17},{9,25},{17,1},{25,9},{2,18},{10... | collective-permute-start | bytes 491528 | tf_op jit(solution)/shard_map/ppermute | solution.py:28
  32.8 9.4 %collective-permute-start.5 = (bf16[2,80,512]{2,1,0:T(8,128)(2,1)S(1)}, bf16[2,80,512]{2,1,0:T(8,128)(2,1)S(1)}, u32[]{:S(2)}, u32[]{:S(2)}) collective-permute-start(bf16[2,80,512]{2,1,0:T(8,128)(2,1)S(1)} %get-tuple-element.31), channel_id=1, source_target_pairs={{0,24},{8,16},{16,8},{24,0},{1,25},{9,17},{17,9},{25,1},{2,26},{10... | collective-permute-start | bytes 491528 | tf_op jit(solution)/shard_map/ppermute | solution.py:28
  35.8 14.7 %collective-permute-start.6 = (bf16[80,1152]{1,0:T(8,128)(2,1)S(1)}, bf16[80,1152]{1,0:T(8,128)(2,1)S(1)}, u32[]{:S(2)}, u32[]{:S(2)}) collective-permute-start(bf16[80,1152]{1,0:T(8,128)(2,1)S(1)} %get-tuple-element.32.acts_ref.refs_4_), channel_id=1, source_target_pairs={{0,8},{8,0},{16,24},{24,16},{1,9},{9,1},{17,25},{25,17},{2,10},{10... | collective-permute-start | bytes 552968 | tf_op jit(solution)/shard_map/ppermute | solution.py:28
  36.2 16.5 %all-to-all-start.1 = ((bf16[8,40,512]{2,1,0:T(8,128)(2,1)}), bf16[8,40,512]{2,1,0:T(8,128)(2,1)S(1)}, u32[]{:S(2)}, u32[]{:S(2)}) async-start(bf16[8,40,512]{2,1,0:T(8,128)(2,1)} %get-tuple-element.27), calls=%async_computation.1 | async-start | bytes 655360 | tf_op jit(solution)/shard_map/all_to_all | solution.py:441
  42.3 4.9 %collective-permute-start.7 = (bf16[80,384]{1,0:T(8,128)(2,1)S(1)}, bf16[80,384]{1,0:T(8,128)(2,1)S(1)}, u32[]{:S(2)}, u32[]{:S(2)}) collective-permute-start(bf16[80,384]{1,0:T(8,128)(2,1)S(1)} %get-tuple-element.33), channel_id=1, source_target_pairs={{0,16},{8,24},{16,0},{24,8},{1,17},{9,25},{17,1},{25,9},{2,18},{10... | collective-permute-start | bytes 184328 | tf_op jit(solution)/shard_map/ppermute | solution.py:28
  43.9 4.7 %collective-permute-start.8 = (bf16[80,384]{1,0:T(8,128)(2,1)S(1)}, bf16[80,384]{1,0:T(8,128)(2,1)S(1)}, u32[]{:S(2)}, u32[]{:S(2)}) collective-permute-start(bf16[80,384]{1,0:T(8,128)(2,1)S(1)} %get-tuple-element.34), channel_id=1, source_target_pairs={{0,16},{8,24},{16,0},{24,8},{1,17},{9,25},{17,1},{25,9},{2,18},{10... | collective-permute-start | bytes 184328 | tf_op jit(solution)/shard_map/ppermute | solution.py:28
  44.4 4.8 %collective-permute-start.9 = (bf16[80,384]{1,0:T(8,128)(2,1)S(1)}, bf16[80,384]{1,0:T(8,128)(2,1)S(1)}, u32[]{:S(2)}, u32[]{:S(2)}) collective-permute-start(bf16[80,384]{1,0:T(8,128)(2,1)S(1)} %get-tuple-element.35), channel_id=1, source_target_pairs={{0,16},{8,24},{16,0},{24,8},{1,17},{9,25},{17,1},{25,9},{2,18},{10... | collective-permute-start | bytes 184328 | tf_op jit(solution)/shard_map/ppermute | solution.py:28
  47.2 2.2 %collective-permute-start.10 = (bf16[80,384]{1,0:T(8,128)(2,1)S(1)}, bf16[80,384]{1,0:T(8,128)(2,1)S(1)}, u32[]{:S(2)}, u32[]{:S(2)}) collective-permute-start(bf16[80,384]{1,0:T(8,128)(2,1)S(1)} %collective-permute-done.7.refs_6_), channel_id=1, source_target_pairs={{0,8},{8,0},{16,24},{24,16},{1,9},{9,1},{17,25},{25,17},{2,10},{10... | collective-permute-start | bytes 184328 | tf_op jit(solution)/shard_map/ppermute | solution.py:28
  48.6 1.2 %collective-permute-start.11 = (bf16[80,384]{1,0:T(8,128)(2,1)S(1)}, bf16[80,384]{1,0:T(8,128)(2,1)S(1)}, u32[]{:S(2)}, u32[]{:S(2)}) collective-permute-start(bf16[80,384]{1,0:T(8,128)(2,1)S(1)} %collective-permute-done.8.refs_7_), channel_id=1, source_target_pairs={{0,8},{8,0},{16,24},{24,16},{1,9},{9,1},{17,25},{25,17},{2,10},{10... | collective-permute-start | bytes 184328 | tf_op jit(solution)/shard_map/ppermute | solution.py:28
  49.2 1.2 %collective-permute-start.12 = (bf16[80,384]{1,0:T(8,128)(2,1)S(1)}, bf16[80,384]{1,0:T(8,128)(2,1)S(1)}, u32[]{:S(2)}, u32[]{:S(2)}) collective-permute-start(bf16[80,384]{1,0:T(8,128)(2,1)S(1)} %collective-permute-done.9.refs_8_), channel_id=1, source_target_pairs={{0,8},{8,0},{16,24},{24,16},{1,9},{9,1},{17,25},{25,17},{2,10},{10... | collective-permute-start | bytes 184328 | tf_op jit(solution)/shard_map/ppermute | solution.py:28
where the time goes:
time: 54.1 us; the launch traced here: 53.9 us
  blocking collectives  23.6 us (44%)
  starting transfers between devices  15.4 us (28%)
  Pallas kernels  8.5 us (16%)
  waiting for transfers between devices  5.52 us (10%)
  between operations  0.79 us (1%)
    all_to_all x1, blocking collectives, on_device(): lax.all_to_all(sent, 'expert', split_axis=0, concat_axis=0, tiled=True)  23.6 us
    ppermute x13, starting transfers between devices, swap(): lax.ppermute(value, 'dp', [(i, i ^ bits) for i in range(lax.axis_size('dp...  9.38 us
    all_to_all x1, starting transfers between devices, on_device(): lax.all_to_all(back, 'expert', split_axis=0, concat_axis=0, tiled=True)  6.05 us
    ppermute x13, waiting for transfers between devices, swap(): lax.ppermute(value, 'dp', [(i, i ^ bits) for i in range(lax.axis_size('dp...  5.19 us
    pallas_call x1, Pallas kernels, on_device(): pl.pallas_call(lambda *refs: back_kernel(groups, *refs), out_shape=(shape...  2.3 us
    pallas_call x1, Pallas kernels, on_device(): pl.pallas_call(lambda *refs: grads_kernel(groups, *refs), out_specs=anywh...  1.89 us
    pallas_call x1, Pallas kernels, on_device(): pl.pallas_call(lambda *refs: partial_kernel(groups, *refs), in_specs=[pl....  1.66 us
    pallas_call x1, Pallas kernels, on_device(): pl.pallas_call(combine_kernel, out_specs=anywhere, out_shape=shape(token_...  1.15 us
  transfers between devices with their start and end apart: 14, of which 7 were waited for; matrix products, arithmetic and copies ran while one was open for 0% of the time, Pallas kernels for 14%

commit v1 on v0

--- a/solution.py
+++ b/solution.py
@@ -126,9 +126,9 @@
 
 
 def part_kernel(acts_ref, *refs):
-    hidden_units = acts_ref.shape[1] // 3
-    for at, ref in enumerate(refs[-3:]):
-        ref[...] = acts_ref[:, at * hidden_units : (at + 1) * hidden_units]
+    wide = refs[-2].shape[1]
+    refs[-2][...] = acts_ref[:, :wide]
+    refs[-1][...] = acts_ref[:, wide:]
 
 
 def keep_kernel(*refs):
@@ -335,7 +335,7 @@
             rows = jnp.concatenate([slices_refs[b][places[b]] for b in some], axis=0)
             acts = jnp.concatenate(
                 [
-                    acts_refs[b][:, lanes] if b < 2 else acts_refs[2 + 3 * (b - 2) + at][...]
+                    acts_refs[2 * b][:, lanes] if at < 2 else acts_refs[2 * b + 1][...]
                     for b in some
                 ],
                 axis=0,
@@ -449,11 +449,11 @@
     parts = pl.pallas_call(
         part_kernel,
         in_specs=[pl.BlockSpec()] + [anywhere] * groups,
-        out_shape=[shape(rows_here, hidden_units)] * 3,
+        out_shape=[shape(rows_here, wide), shape(rows_here, hidden_units)],
         compiler_params=params(acts, acts),
         cost_estimate=cost(10**6, 10**5),
     )(acts, later, *slices[1:])
-    every = slices + [acts, swap(acts, 1)]
+    every = slices + list(parts) + [swap(part, 1) for part in parts]
     for b in far:
         over = [swap(part, b) for part in parts]
         every += over + [swap(part, 1) for part in over]

time: 54.1 us -> 54.1 us (level)
  starting transfers between devices: 15.4 us -> 13.9 us
  waiting for transfers between devices: 5.52 us -> 7 us
    ppermute x13 -> x12, starting transfers between devices: 9.38 us -> 7.99 us  [swap(): lax.ppermute(value, 'dp', [(i, i ^ bits) for i in range(lax.axis_size('dp...]
    ppermute x13 -> x12, waiting for transfers between devices: 5.19 us -> 6.1 us  [swap(): lax.ppermute(value, 'dp', [(i, i ^ bits) for i in range(lax.axis_size('dp...]
    all_to_all x1, waiting for transfers between devices: 0.33 us -> 0.9 us  [on_device(): lax.all_to_all(back, 'expert', split_axis=0, concat_axis=0, tiled=True)]
  transfers between devices with their start and end apart: 14 -> 13, of which waited for: 7 -> 6; matrix products, arithmetic and copies ran while one was open for 0% -> 0% of each run, Pallas kernels for 14% -> 14%
where the time goes in v1:
time: 54.1 us; the launch traced here: 53.8 us
  blocking collectives  23.6 us (44%)
  starting transfers between devices  13.9 us (26%)
  Pallas kernels  8.49 us (16%)
  waiting for transfers between devices  7 us (13%)
  between operations  0.78 us (1%)
    all_to_all x1, blocking collectives, on_device(): lax.all_to_all(sent, 'expert', split_axis=0, concat_axis=0, tiled=True)  23.6 us
    ppermute x12, starting transfers between devices, swap(): lax.ppermute(value, 'dp', [(i, i ^ bits) for i in range(lax.axis_size('dp...  7.99 us
    ppermute x12, waiting for transfers between devices, swap(): lax.ppermute(value, 'dp', [(i, i ^ bits) for i in range(lax.axis_size('dp...  6.1 us
    all_to_all x1, starting transfers between devices, on_device(): lax.all_to_all(back, 'expert', split_axis=0, concat_axis=0, tiled=True)  5.94 us
    pallas_call x1, Pallas kernels, on_device(): pl.pallas_call(lambda *refs: back_kernel(groups, *refs), out_shape=(shape...  2.3 us
    pallas_call x1, Pallas kernels, on_device(): pl.pallas_call(lambda *refs: grads_kernel(groups, *refs), out_specs=anywh...  1.89 us
    pallas_call x1, Pallas kernels, on_device(): pl.pallas_call(lambda *refs: partial_kernel(groups, *refs), in_specs=[pl....  1.66 us
    pallas_call x1, Pallas kernels, on_device(): pl.pallas_call(combine_kernel, out_specs=anywhere, out_shape=shape(token_...  1.15 us
  transfers between devices with their start and end apart: 13, of which 6 were waited for; matrix products, arithmetic and copies ran while one was open for 0% of the time, Pallas kernels for 14%

profile of v1, /device:TPU:0, one launch (start us, length us, event | category | flops | bytes accessed | tf_op | source)
XLA Modules:
  0.0 53.8 jit_solution(6174746554904638419)
XLA Ops:
  0.7 0.5 collective-permute-start
  1.2 2.6 %collective-permute-start.1 = (bf16[1,3,512,384]{3,2,1,0:T(8,128)(2,1)}, bf16[1,3,512,384]{3,2,1,0:T(8,128)(2,1)S(1)}, u32[]{:S(2)}, u32[]{:S(2)}) collective-permute-start(bf16[1,3,512,384]{3,2,1,0:T(8,128)(2,1)} %refs_1_.1), channel_id=1, source_target_pairs={{0,16},{8,24},{16,0},{24,8},{1,17},{9,25},{17,1},{25,9},{2,18},{10... | collective-permute-start | bytes 3538952 | tf_op jit(solution)/shard_map/ppermute | solution.py:28
  3.8 0.0 copy-start
  3.8 0.6 %shard_map.69 = (bf16[8,80,512]{2,1,0:T(8,128)(2,1)S(1)}, f32[8,128]{1,0:T(8,128)S(1)}) custom-call(s32[8,128]{1,0:T(8,128)S(1)} %bitcast.2, bf16[8,128]{1,0:T(8,128)(2,1)S(1)} %bitcast.3, bf16[128,2048]{1,0:T(8,128)(2,1)S(1)} %copy-done.1, bf16[128,2048]{1,0:T(8,128)(2,1)S(1)} %copy-done.2, f32[8,128]{1,0:T(8,128)S(1)} %shard_map.68._), custom_call_target="tpu_custom_call" | custom-call | tf_op jit(solution)/shard_map/pallas_call | solution.py:374
  4.5 23.6 %all_to_all.10.refs_0_ = bf16[8,80,512]{2,1,0:T(8,128)(2,1)S(1)} all-to-all(bf16[8,80,512]{2,1,0:T(8,128)(2,1)S(1)} %get-tuple-element.18), channel_id=1, replica_groups=mesh['dp'=4,'expert'=8] {'expert'}, dimensions={0} | all-to-all | bytes 1310720 | tf_op jit(solution)/shard_map/all_to_all | solution.py:383
  28.1 0.0 collective-permute-done.refs_2_
  28.1 1.7 %shard_map.70 = (f32[80,1152]{1,0:T(8,128)S(1)}, bf16[80,2048]{1,0:T(8,128)(2,1)S(1)}, bf16[80,2048]{1,0:T(8,128)(2,1)S(1)}, bf16[2,512,768]{2,1,0:T(8,128)(2,1)...) custom-call(bf16[8,80,512]{2,1,0:T(8,128)(2,1)S(1)} %all_to_all.10.r, ...), custom_call_target="tpu_custom_call" | custom-call | tf_op jit(solution)/shard_map/pallas_call | solution.py:391
  29.7 0.8 %collective-permute-done.1.refs_1_ = bf16[1,3,512,384]{3,2,1,0:T(8,128)(2,1)S(1)} collective-permute-done((bf16[1,3,512,384]{3,2,1,0:T(8,128)(2,1)}, bf16[1,3,512,384]{3,2,1,0:T(8,128)(2,1)S(1)}, u32[]{:S(2)}, u32[]{:S(2)}) %collective-permute-start.1) | collective-permute-done | bytes 1179680 | tf_op jit(solution)/shard_map/ppermute | solution.py:28
  30.6 0.0 collective-permute-start.2
  30.6 0.5 collective-permute-start.3
  31.1 1.8 %collective-permute-start.4 = (bf16[2,80,512]{2,1,0:T(8,128)(2,1)S(1)}, bf16[2,80,512]{2,1,0:T(8,128)(2,1)S(1)}, u32[]{:S(2)}, u32[]{:S(2)}) collective-permute-start(bf16[2,80,512]{2,1,0:T(8,128)(2,1)S(1)} %get-tuple-element.29), channel_id=1, source_target_pairs={{0,16},{8,24},{16,0},{24,8},{1,17},{9,25},{17,1},{25,9},{2,18},{10... | collective-permute-start | bytes 491528 | tf_op jit(solution)/shard_map/ppermute | solution.py:28
  32.8 0.0 collective-permute-start.5
  32.8 0.7 %shard_map.72 = (f32[80,1152]{1,0:T(8,128)S(1)}, bf16[1,512,768]{2,1,0:T(8,128)(2,1)S(1)}) custom-call(bf16[80,2048]{1,0:T(8,128)(2,1)S(1)} %get-tuple-element.19.refs_0_, bf16[80,2048]{1,0:T(8,128)(2,1)S(1)} %get-tuple-element.20.refs_1_, f32[80,1152]{1,0:T(8,128)S(1)} %get-tuple-element.21.refs_2_, bf16[1,3,512,384]{3,2,1,0:T(8,128)(2,1)S(1)} %shard_map.71.refs_3_), custom_call_target="tpu_custom_call" | custom-call | tf_op jit(solution)/shard_map/pallas_call | solution.py:423
  33.5 0.0 collective-permute-done.2.refs_5_
  33.5 2.3 %shard_map.73 = (bf16[80,1152]{1,0:T(8,128)(2,1)S(1)}, bf16[8,40,512]{2,1,0:T(8,128)(2,1)}) custom-call(bf16[80,2048]{1,0:T(8,128)(2,1)S(1)} %get-tuple-element.19.refs_0_, bf16[80,2048]{1,0:T(8,128)(2,1)S(1)} %get-tuple-element.20.refs_1_, f32[80,1152]{1,0:T(8,128)S(1)} %get-tuple-element.23.refs_2_, bf16[2,512,768]{2,1,0:T(8,128)(2,1)S(1)} %get-tuple-element.24.refs_3_, ...), custom_call_target="tpu_custom_call" | custom-call | flops 1000000 | bytes 100000 | tf_op jit(solution)/shard_map/pallas_call | solution.py:434
  35.8 5.9 %all-to-all-start.1 = ((bf16[8,40,512]{2,1,0:T(8,128)(2,1)}), bf16[8,40,512]{2,1,0:T(8,128)(2,1)S(1)}, u32[]{:S(2)}, u32[]{:S(2)}) async-start(bf16[8,40,512]{2,1,0:T(8,128)(2,1)} %get-tuple-element.26), calls=%async_computation.1 | async-start | bytes 655360 | tf_op jit(solution)/shard_map/all_to_all | solution.py:441
  41.8 0.0 collective-permute-done.5.refs_3_
  41.8 0.0 collective-permute-done.3.refs_1_
  41.8 1.6 %collective-permute-start.8 = (bf16[80,768]{1,0:T(8,128)(2,1)S(1)}, bf16[80,768]{1,0:T(8,128)(2,1)S(1)}, u32[]{:S(2)}, u32[]{:S(2)}) collective-permute-start(bf16[80,768]{1,0:T(8,128)(2,1)S(1)} %get-tuple-element.32.refs_4_), channel_id=1, source_target_pairs={{0,16},{8,24},{16,0},{24,8},{1,17},{9,25},{17,1},{25,9},{2,18},{10... | collective-permute-start | bytes 368648 | tf_op jit(solution)/shard_map/ppermute | solution.py:28
  43.4 0.0 collective-permute-start.6
  43.4 0.5 collective-permute-start.9
  43.9 4.1 %collective-permute-done.8.refs_8_ = bf16[80,768]{1,0:T(8,128)(2,1)S(1)} collective-permute-done((bf16[80,768]{1,0:T(8,128)(2,1)S(1)}, bf16[80,768]{1,0:T(8,128)(2,1)S(1)}, u32[]{:S(2)}, u32[]{:S(2)}) %collective-permute-start.8) | collective-permute-done | bytes 122912 | tf_op jit(solution)/shard_map/ppermute | solution.py:28
  48.0 0.0 collective-permute-start.10
  48.0 0.5 collective-permute-start.7
  48.5 0.1 collective-permute-done.9.refs_9_
  48.6 0.2 shard_map.74.table_ref
  48.8 0.6 %collective-permute-done.7.refs_7_ = bf16[80,384]{1,0:T(8,128)(2,1)S(1)} collective-permute-done((bf16[80,384]{1,0:T(8,128)(2,1)S(1)}, bf16[80,384]{1,0:T(8,128)(2,1)S(1)}, u32[]{:S(2)}, u32[]{:S(2)}) %collective-permute-start.7) | collective-permute-done | bytes 61472 | tf_op jit(solution)/shard_map/ppermute | solution.py:28
  49.4 0.5 collective-permute-done.11.refs_11_
  49.9 0.0 collective-permute-done.10.refs_10_
  49.9 1.9 %shard_map.78 = f32[1,3,512,384]{3,2,1,0:T(8,128)} custom-call(bf16[4,80,512]{2,1,0:T(8,128)(2,1)S(1)} %get-tuple-element.28.refs_0_, bf16[4,80,512]{2,1,0:T(8,128)(2,1)S(1)} %collective-permute-done.3.refs_1_, bf16[2,80,512]{2,1,0:T(8,128)(2,1)S(1)} %collective-permute-done.4.refs_2_, bf16[2,80,512]{2,1,0:T(8,128)(2,1)S(1)} %collective-permute-done.5.refs_3_, ...), custom_call_target="tpu_custom_call" | custom-call | flops 377487360 | bytes 2359296 | tf_op jit(solution)/shard_map/pallas_call | solution.py:460
  51.8 0.9 %all-to-all-done.1.returned_ref = bf16[8,40,512]{2,1,0:T(8,128)(2,1)S(1)} async-done(((bf16[8,40,512]{2,1,0:T(8,128)(2,1)}), bf16[8,40,512]{2,1,0:T(8,128)(2,1)S(1)}, u32[]{:S(2)}, u32[]{:S(2)}) %all-to-all-start.1) | async-done | bytes 327712 | tf_op jit(solution)/shard_map/all_to_all | solution.py:441
  52.7 1.1 %shard_map.75 = bf16[128,2048]{1,0:T(8,128)(2,1)} custom-call(bf16[8,40,512]{2,1,0:T(8,128)(2,1)S(1)} %all-to-all-done.1.returned_ref, bf16[512,320]{1,0:T(8,128)(2,1)S(1)} %shard_map.74.table_ref), custom_call_target="tpu_custom_call" | custom-call | tf_op jit(solution)/shard_map/pallas_call | solution.py:472
  (16 shorter events, 0.0 us)
Async XLA Ops:
  0.6 3.2 %copy-start.3 = (s32[128,8]{0,1:T(8,128)S(1)}, s32[128,8]{0,1:T(8,128)}, u32[]{:S(2)}) copy-start(s32[128,8]{0,1:T(8,128)} %param.7) | copy-start | bytes 12292
  0.6 3.2 %copy-start.4 = (bf16[128,8]{0,1:T(8,128)(2,1)S(1)}, bf16[128,8]{0,1:T(8,128)(2,1)}, u32[]{:S(2)}) copy-start(bf16[128,8]{0,1:T(8,128)(2,1)} %param.8) | copy-start | bytes 6148
  0.7 3.1 %copy-start.1 = (bf16[128,2048]{1,0:T(8,128)(2,1)S(1)}, bf16[128,2048]{1,0:T(8,128)(2,1)}, u32[]{:S(2)}) copy-start(bf16[128,2048]{1,0:T(8,128)(2,1)} %tokens_ref.1) | copy-start | bytes 1572868
  0.7 3.1 %copy-start.2 = (bf16[128,2048]{1,0:T(8,128)(2,1)S(1)}, bf16[128,2048]{1,0:T(8,128)(2,1)}, u32[]{:S(2)}) copy-start(bf16[128,2048]{1,0:T(8,128)(2,1)} %grads_ref.1) | copy-start | bytes 1572868
  0.7 27.4 %collective-permute-start = (bf16[1,3,512,384]{3,2,1,0:T(8,128)(2,1)}, bf16[1,3,512,384]{3,2,1,0:T(8,128)(2,1)S(1)}, u32[]{:S(2)}, u32[]{:S(2)}) collective-permute-start(bf16[1,3,512,384]{3,2,1,0:T(8,128)(2,1)} %refs_1_.1), channel_id=1, source_target_pairs={{0,8},{8,0},{16,24},{24,16},{1,9},{9,1},{17,25},{25,17},{2,10},{10... | collective-permute-start | bytes 3538952 | tf_op jit(solution)/shard_map/ppermute | solution.py:28
  1.2 29.4 %collective-permute-start.1 = (bf16[1,3,512,384]{3,2,1,0:T(8,128)(2,1)}, bf16[1,3,512,384]{3,2,1,0:T(8,128)(2,1)S(1)}, u32[]{:S(2)}, u32[]{:S(2)}) collective-permute-start(bf16[1,3,512,384]{3,2,1,0:T(8,128)(2,1)} %refs_1_.1), channel_id=1, source_target_pairs={{0,16},{8,24},{16,0},{24,8},{1,17},{9,25},{17,1},{25,9},{2,18},{10... | collective-permute-start | bytes 3538952 | tf_op jit(solution)/shard_map/ppermute | solution.py:28
  3.8 24.3 %copy-start = (bf16[1,3,512,384]{3,2,1,0:T(8,128)(2,1)S(1)}, bf16[1,3,512,384]{3,2,1,0:T(8,128)(2,1)}, u32[]{:S(2)}) copy-start(bf16[1,3,512,384]{3,2,1,0:T(8,128)(2,1)} %refs_1_.1) | copy-start | bytes 3538948
  30.6 2.9 %collective-permute-start.2 = (bf16[1,3,512,384]{3,2,1,0:T(8,128)(2,1)S(1)}, bf16[1,3,512,384]{3,2,1,0:T(8,128)(2,1)S(1)}, u32[]{:S(2)}, u32[]{:S(2)}) collective-permute-start(bf16[1,3,512,384]{3,2,1,0:T(8,128)(2,1)S(1)} %shard_map.71.refs_3_), channel_id=1, source_target_pairs={{0,8},{8,0},{16,24},{24,16},{1,9},{9,1},{17,25},{25,17},{2,10},{10... | collective-permute-start | bytes 3538952 | tf_op jit(solution)/shard_map/ppermute | solution.py:28
  30.6 11.2 %collective-permute-start.3 = (bf16[4,80,512]{2,1,0:T(8,128)(2,1)S(1)}, bf16[4,80,512]{2,1,0:T(8,128)(2,1)S(1)}, u32[]{:S(2)}, u32[]{:S(2)}) collective-permute-start(bf16[4,80,512]{2,1,0:T(8,128)(2,1)S(1)} %get-tuple-element.28.refs_0_), channel_id=1, source_target_pairs={{0,8},{8,0},{16,24},{24,16},{1,9},{9,1},{17,25},{25,17},{2,10},{10... | collective-permute-start | bytes 983048 | tf_op jit(solution)/shard_map/ppermute | solution.py:28
  31.1 10.7 %collective-permute-start.4 = (bf16[2,80,512]{2,1,0:T(8,128)(2,1)S(1)}, bf16[2,80,512]{2,1,0:T(8,128)(2,1)S(1)}, u32[]{:S(2)}, u32[]{:S(2)}) collective-permute-start(bf16[2,80,512]{2,1,0:T(8,128)(2,1)S(1)} %get-tuple-element.29), channel_id=1, source_target_pairs={{0,16},{8,24},{16,0},{24,8},{1,17},{9,25},{17,1},{25,9},{2,18},{10... | collective-permute-start | bytes 491528 | tf_op jit(solution)/shard_map/ppermute | solution.py:28
  32.8 8.9 %collective-permute-start.5 = (bf16[2,80,512]{2,1,0:T(8,128)(2,1)S(1)}, bf16[2,80,512]{2,1,0:T(8,128)(2,1)S(1)}, u32[]{:S(2)}, u32[]{:S(2)}) collective-permute-start(bf16[2,80,512]{2,1,0:T(8,128)(2,1)S(1)} %get-tuple-element.30), channel_id=1, source_target_pairs={{0,24},{8,16},{16,8},{24,0},{1,25},{9,17},{17,9},{25,1},{2,26},{10... | collective-permute-start | bytes 491528 | tf_op jit(solution)/shard_map/ppermute | solution.py:28
  35.8 16.9 %all-to-all-start.1 = ((bf16[8,40,512]{2,1,0:T(8,128)(2,1)}), bf16[8,40,512]{2,1,0:T(8,128)(2,1)S(1)}, u32[]{:S(2)}, u32[]{:S(2)}) async-start(bf16[8,40,512]{2,1,0:T(8,128)(2,1)} %get-tuple-element.26), calls=%async_computation.1 | async-start | bytes 655360 | tf_op jit(solution)/shard_map/all_to_all | solution.py:441
  41.8 6.2 %collective-permute-start.8 = (bf16[80,768]{1,0:T(8,128)(2,1)S(1)}, bf16[80,768]{1,0:T(8,128)(2,1)S(1)}, u32[]{:S(2)}, u32[]{:S(2)}) collective-permute-start(bf16[80,768]{1,0:T(8,128)(2,1)S(1)} %get-tuple-element.32.refs_4_), channel_id=1, source_target_pairs={{0,16},{8,24},{16,0},{24,8},{1,17},{9,25},{17,1},{25,9},{2,18},{10... | collective-permute-start | bytes 368648 | tf_op jit(solution)/shard_map/ppermute | solution.py:28
  43.4 6.0 %collective-permute-start.6 = (bf16[80,768]{1,0:T(8,128)(2,1)S(1)}, bf16[80,768]{1,0:T(8,128)(2,1)S(1)}, u32[]{:S(2)}, u32[]{:S(2)}) collective-permute-start(bf16[80,768]{1,0:T(8,128)(2,1)S(1)} %get-tuple-element.32.refs_4_), channel_id=1, source_target_pairs={{0,8},{8,0},{16,24},{24,16},{1,9},{9,1},{17,25},{25,17},{2,10},{10... | collective-permute-start | bytes 368648 | tf_op jit(solution)/shard_map/ppermute | solution.py:28
  43.4 5.2 %collective-permute-start.9 = (bf16[80,384]{1,0:T(8,128)(2,1)S(1)}, bf16[80,384]{1,0:T(8,128)(2,1)S(1)}, u32[]{:S(2)}, u32[]{:S(2)}) collective-permute-start(bf16[80,384]{1,0:T(8,128)(2,1)S(1)} %get-tuple-element.33.refs_5_), channel_id=1, source_target_pairs={{0,16},{8,24},{16,0},{24,8},{1,17},{9,25},{17,1},{25,9},{2,18},{10... | collective-permute-start | bytes 184328 | tf_op jit(solution)/shard_map/ppermute | solution.py:28
  48.0 1.9 %collective-permute-start.10 = (bf16[80,768]{1,0:T(8,128)(2,1)S(1)}, bf16[80,768]{1,0:T(8,128)(2,1)S(1)}, u32[]{:S(2)}, u32[]{:S(2)}) collective-permute-start(bf16[80,768]{1,0:T(8,128)(2,1)S(1)} %collective-permute-done.8.refs_8_), channel_id=1, source_target_pairs={{0,8},{8,0},{16,24},{24,16},{1,9},{9,1},{17,25},{25,17},{2,10},{10... | collective-permute-start | bytes 368648 | tf_op jit(solution)/shard_map/ppermute | solution.py:28
  48.0 1.4 %collective-permute-start.7 = (bf16[80,384]{1,0:T(8,128)(2,1)S(1)}, bf16[80,384]{1,0:T(8,128)(2,1)S(1)}, u32[]{:S(2)}, u32[]{:S(2)}) collective-permute-start(bf16[80,384]{1,0:T(8,128)(2,1)S(1)} %get-tuple-element.33.refs_5_), channel_id=1, source_target_pairs={{0,8},{8,0},{16,24},{24,16},{1,9},{9,1},{17,25},{25,17},{2,10},{10... | collective-permute-start | bytes 184328 | tf_op jit(solution)/shard_map/ppermute | solution.py:28
  48.6 1.2 %collective-permute-start.11 = (bf16[80,384]{1,0:T(8,128)(2,1)S(1)}, bf16[80,384]{1,0:T(8,128)(2,1)S(1)}, u32[]{:S(2)}, u32[]{:S(2)}) collective-permute-start(bf16[80,384]{1,0:T(8,128)(2,1)S(1)} %collective-permute-done.9.refs_9_), channel_id=1, source_target_pairs={{0,8},{8,0},{16,24},{24,16},{1,9},{9,1},{17,25},{25,17},{2,10},{10... | collective-permute-start | bytes 184328 | tf_op jit(solution)/shard_map/ppermute | solution.py:28

commit v2 on v1

--- a/solution.py
+++ b/solution.py
@@ -125,10 +125,12 @@
     table_ref[...] = table.T.astype(BF16)
 
 
-def part_kernel(acts_ref, *refs):
-    wide = refs[-2].shape[1]
-    refs[-2][...] = acts_ref[:, :wide]
-    refs[-1][...] = acts_ref[:, wide:]
+def part_kernel(acts_ref, local_ref, *refs):
+    pair_ref, hidden_ref, near_ref = refs[-3:]
+    wide = pair_ref.shape[1]
+    pair_ref[...] = acts_ref[:, :wide]
+    hidden_ref[...] = acts_ref[:, wide:]
+    near_ref[...] = local_ref[:2]
 
 
 def keep_kernel(*refs):
@@ -408,7 +410,7 @@
     )(got, expert_weights, near)
     partial, rows, grads, near_pairs, token = outs[:5]
     slices = list(outs[5:])
-    slices = slices[:1] + [swap(slices[b - 1], b) for b in range(1, groups)]
+    local, slices = slices[0], [swap(slices[b - 1], b) for b in range(2, groups)]
 
     arrived = pl.pallas_call(
         keep_kernel,
@@ -446,14 +448,18 @@
         compiler_params=params(),
         cost_estimate=cost(10**11, 10**8),
     )()
-    parts = pl.pallas_call(
+    *parts, beside = pl.pallas_call(
         part_kernel,
-        in_specs=[pl.BlockSpec()] + [anywhere] * groups,
-        out_shape=[shape(rows_here, wide), shape(rows_here, hidden_units)],
-        compiler_params=params(acts, acts),
+        in_specs=[pl.BlockSpec()] * 2 + [anywhere] * (groups - 1),
+        out_shape=[
+            shape(rows_here, wide),
+            shape(rows_here, hidden_units),
+            shape(2, rows_here, owned),
+        ],
+        compiler_params=params(acts, acts, local),
         cost_estimate=cost(10**6, 10**5),
-    )(acts, later, *slices[1:])
-    every = slices + list(parts) + [swap(part, 1) for part in parts]
+    )(acts, local, later, *slices)
+    every = [local, swap(beside, 1)] + slices + parts + [swap(part, 1) for part in parts]
     for b in far:
         over = [swap(part, b) for part in parts]
         every += over + [swap(part, 1) for part in over]

time: 54.1 us -> 53.7 us (level)
  waiting for transfers between devices: 7 us -> 6.41 us
    ppermute x12, waiting for transfers between devices: 6.1 us -> 5.51 us  [swap(): lax.ppermute(value, 'dp', [(i, i ^ bits) for i in range(lax.axis_size('dp...]
  transfers between devices with their start and end apart: 13 -> 13, of which waited for: 6 -> 7; matrix products, arithmetic and copies ran while one was open for 0% -> 0% of each run, Pallas kernels for 14% -> 14%
where the time goes in v2:
time: 53.7 us; the launch traced here: 53.5 us
  blocking collectives  23.6 us (44%)
  starting transfers between devices  14.2 us (26%)
  Pallas kernels  8.51 us (16%)
  waiting for transfers between devices  6.41 us (12%)
  between operations  0.76 us (1%)
    all_to_all x1, blocking collectives, on_device(): lax.all_to_all(sent, 'expert', split_axis=0, concat_axis=0, tiled=True)  23.6 us
    ppermute x12, starting transfers between devices, swap(): lax.ppermute(value, 'dp', [(i, i ^ bits) for i in range(lax.axis_size('dp...  8.13 us
    all_to_all x1, starting transfers between devices, on_device(): lax.all_to_all(back, 'expert', split_axis=0, concat_axis=0, tiled=True)  6.04 us
    ppermute x12, waiting for transfers between devices, swap(): lax.ppermute(value, 'dp', [(i, i ^ bits) for i in range(lax.axis_size('dp...  5.51 us
    pallas_call x1, Pallas kernels, on_device(): pl.pallas_call(lambda *refs: back_kernel(groups, *refs), out_shape=(shape...  2.3 us
    pallas_call x1, Pallas kernels, on_device(): pl.pallas_call(lambda *refs: grads_kernel(groups, *refs), out_specs=anywh...  1.89 us
    pallas_call x1, Pallas kernels, on_device(): pl.pallas_call(lambda *refs: partial_kernel(groups, *refs), in_specs=[pl....  1.66 us
    pallas_call x1, Pallas kernels, on_device(): pl.pallas_call(combine_kernel, out_specs=anywhere, out_shape=shape(token_...  1.15 us
  transfers between devices with their start and end apart: 13, of which 7 were waited for; matrix products, arithmetic and copies ran while one was open for 0% of the time, Pallas kernels for 14%

profile of v2, /device:TPU:0, one launch (start us, length us, event | category | flops | bytes accessed | tf_op | source)
XLA Modules:
  0.0 53.5 jit_solution(6238244413706462225)
XLA Ops:
  0.7 0.5 collective-permute-start
  1.2 2.6 %collective-permute-start.1 = (bf16[1,3,512,384]{3,2,1,0:T(8,128)(2,1)}, bf16[1,3,512,384]{3,2,1,0:T(8,128)(2,1)S(1)}, u32[]{:S(2)}, u32[]{:S(2)}) collective-permute-start(bf16[1,3,512,384]{3,2,1,0:T(8,128)(2,1)} %refs_1_.1), channel_id=1, source_target_pairs={{0,16},{8,24},{16,0},{24,8},{1,17},{9,25},{17,1},{25,9},{2,18},{10... | collective-permute-start | bytes 3538952 | tf_op jit(solution)/shard_map/ppermute | solution.py:28
  3.8 0.0 copy-start
  3.8 0.6 %shard_map.69 = (bf16[8,80,512]{2,1,0:T(8,128)(2,1)S(1)}, f32[8,128]{1,0:T(8,128)S(1)}) custom-call(s32[8,128]{1,0:T(8,128)S(1)} %bitcast.2, bf16[8,128]{1,0:T(8,128)(2,1)S(1)} %bitcast.3, bf16[128,2048]{1,0:T(8,128)(2,1)S(1)} %copy-done.1, bf16[128,2048]{1,0:T(8,128)(2,1)S(1)} %copy-done.2, f32[8,128]{1,0:T(8,128)S(1)} %shard_map.68._), custom_call_target="tpu_custom_call" | custom-call | tf_op jit(solution)/shard_map/pallas_call | solution.py:376
  4.5 23.6 %all_to_all.10.refs_0_ = bf16[8,80,512]{2,1,0:T(8,128)(2,1)S(1)} all-to-all(bf16[8,80,512]{2,1,0:T(8,128)(2,1)S(1)} %get-tuple-element.19), channel_id=1, replica_groups=mesh['dp'=4,'expert'=8] {'expert'}, dimensions={0} | all-to-all | bytes 1310720 | tf_op jit(solution)/shard_map/all_to_all | solution.py:385
  28.1 0.0 collective-permute-done.refs_2_
  28.1 1.7 %shard_map.70 = (f32[80,1152]{1,0:T(8,128)S(1)}, bf16[80,2048]{1,0:T(8,128)(2,1)S(1)}, bf16[80,2048]{1,0:T(8,128)(2,1)S(1)}, bf16[2,512,768]{2,1,0:T(8,128)(2,1)...) custom-call(bf16[8,80,512]{2,1,0:T(8,128)(2,1)S(1)} %all_to_all.10.r, ...), custom_call_target="tpu_custom_call" | custom-call | tf_op jit(solution)/shard_map/pallas_call | solution.py:393
  29.7 0.8 %collective-permute-done.1.refs_1_ = bf16[1,3,512,384]{3,2,1,0:T(8,128)(2,1)S(1)} collective-permute-done((bf16[1,3,512,384]{3,2,1,0:T(8,128)(2,1)}, bf16[1,3,512,384]{3,2,1,0:T(8,128)(2,1)S(1)}, u32[]{:S(2)}, u32[]{:S(2)}) %collective-permute-start.1) | collective-permute-done | bytes 1179680 | tf_op jit(solution)/shard_map/ppermute | solution.py:28
  30.6 0.0 collective-permute-start.2
  30.6 1.8 %collective-permute-start.3 = (bf16[2,80,512]{2,1,0:T(8,128)(2,1)S(1)}, bf16[2,80,512]{2,1,0:T(8,128)(2,1)S(1)}, u32[]{:S(2)}, u32[]{:S(2)}) collective-permute-start(bf16[2,80,512]{2,1,0:T(8,128)(2,1)S(1)} %get-tuple-element.31), channel_id=1, source_target_pairs={{0,16},{8,24},{16,0},{24,8},{1,17},{9,25},{17,1},{25,9},{2,18},{10... | collective-permute-start | bytes 491528 | tf_op jit(solution)/shard_map/ppermute | solution.py:28
  32.3 0.1 collective-permute-start.4
  32.5 0.7 %shard_map.72 = (f32[80,1152]{1,0:T(8,128)S(1)}, bf16[1,512,768]{2,1,0:T(8,128)(2,1)S(1)}) custom-call(bf16[80,2048]{1,0:T(8,128)(2,1)S(1)} %get-tuple-element.20.refs_0_, bf16[80,2048]{1,0:T(8,128)(2,1)S(1)} %get-tuple-element.21.refs_1_, f32[80,1152]{1,0:T(8,128)S(1)} %get-tuple-element.22.refs_2_, bf16[1,3,512,384]{3,2,1,0:T(8,128)(2,1)S(1)} %shard_map.71.refs_3_), custom_call_target="tpu_custom_call" | custom-call | tf_op jit(solution)/shard_map/pallas_call | solution.py:425
  33.1 0.3 collective-permute-done.2.refs_5_
  33.4 2.3 %shard_map.73 = (bf16[80,1152]{1,0:T(8,128)(2,1)S(1)}, bf16[8,40,512]{2,1,0:T(8,128)(2,1)}) custom-call(bf16[80,2048]{1,0:T(8,128)(2,1)S(1)} %get-tuple-element.20.refs_0_, bf16[80,2048]{1,0:T(8,128)(2,1)S(1)} %get-tuple-element.21.refs_1_, f32[80,1152]{1,0:T(8,128)S(1)} %get-tuple-element.24.refs_2_, bf16[2,512,768]{2,1,0:T(8,128)(2,1)S(1)} %get-tuple-element.25.refs_3_, ...), custom_call_target="tpu_custom_call" | custom-call | flops 1000000 | bytes 100000 | tf_op jit(solution)/shard_map/pallas_call | solution.py:436
  35.7 6.0 %all-to-all-start.1 = ((bf16[8,40,512]{2,1,0:T(8,128)(2,1)}), bf16[8,40,512]{2,1,0:T(8,128)(2,1)S(1)}, u32[]{:S(2)}, u32[]{:S(2)}) async-start(bf16[8,40,512]{2,1,0:T(8,128)(2,1)} %get-tuple-element.27), calls=%async_computation.1 | async-start | bytes 655360 | tf_op jit(solution)/shard_map/all_to_all | solution.py:443
  41.8 0.0 collective-permute-done.3.refs_1_.refs_2_
  41.8 0.0 collective-permute-done.4.refs_2_.refs_3_
  41.8 1.6 %collective-permute-start.8 = (bf16[80,768]{1,0:T(8,128)(2,1)S(1)}, bf16[80,768]{1,0:T(8,128)(2,1)S(1)}, u32[]{:S(2)}, u32[]{:S(2)}) collective-permute-start(bf16[80,768]{1,0:T(8,128)(2,1)S(1)} %get-tuple-element.34.refs_4_), channel_id=1, source_target_pairs={{0,16},{8,24},{16,0},{24,8},{1,17},{9,25},{17,1},{25,9},{2,18},{10... | collective-permute-start | bytes 368648 | tf_op jit(solution)/shard_map/ppermute | solution.py:28
  43.4 0.0 collective-permute-start.5
  43.4 0.5 collective-permute-start.6
  43.9 0.5 collective-permute-start.9
  44.4 3.0 %collective-permute-done.8.refs_8_ = bf16[80,768]{1,0:T(8,128)(2,1)S(1)} collective-permute-done((bf16[80,768]{1,0:T(8,128)(2,1)S(1)}, bf16[80,768]{1,0:T(8,128)(2,1)S(1)}, u32[]{:S(2)}, u32[]{:S(2)}) %collective-permute-start.8) | collective-permute-done | bytes 122912 | tf_op jit(solution)/shard_map/ppermute | solution.py:28
  47.4 0.5 collective-permute-start.7
  47.9 0.4 collective-permute-done.9.refs_9_
  48.3 0.2 shard_map.74.table_ref
  48.5 0.4 collective-permute-done.7.refs_7_
  48.8 0.0 collective-permute-done.6.refs_6_
  48.8 0.7 %collective-permute-done.11.refs_11_ = bf16[80,384]{1,0:T(8,128)(2,1)S(1)} collective-permute-done((bf16[80,384]{1,0:T(8,128)(2,1)S(1)}, bf16[80,384]{1,0:T(8,128)(2,1)S(1)}, u32[]{:S(2)}, u32[]{:S(2)}) %collective-permute-start.11) | collective-permute-done | bytes 61472 | tf_op jit(solution)/shard_map/ppermute | solution.py:28
  49.5 0.0 collective-permute-done.5.refs_1_
  49.5 1.9 %shard_map.78 = f32[1,3,512,384]{3,2,1,0:T(8,128)} custom-call(bf16[4,80,512]{2,1,0:T(8,128)(2,1)S(1)} %get-tuple-element.29.local_ref.refs_0_, bf16[2,80,512]{2,1,0:T(8,128)(2,1)S(1)} %collective-permute-done.5.refs_1_, bf16[2,80,512]{2,1,0:T(8,128)(2,1)S(1)} %collective-permute-done.3.refs_1_.refs_2_, ...), custom_call_target="tpu_custom_call" | custom-call | flops 377487360 | bytes 2359296 | tf_op jit(solution)/shard_map/pallas_call | solution.py:466
  51.4 0.9 %all-to-all-done.1.returned_ref = bf16[8,40,512]{2,1,0:T(8,128)(2,1)S(1)} async-done(((bf16[8,40,512]{2,1,0:T(8,128)(2,1)}), bf16[8,40,512]{2,1,0:T(8,128)(2,1)S(1)}, u32[]{:S(2)}, u32[]{:S(2)}) %all-to-all-start.1) | async-done | bytes 327712 | tf_op jit(solution)/shard_map/all_to_all | solution.py:443
  52.3 1.2 %shard_map.75 = bf16[128,2048]{1,0:T(8,128)(2,1)} custom-call(bf16[8,40,512]{2,1,0:T(8,128)(2,1)S(1)} %all-to-all-done.1.returned_ref, bf16[512,320]{1,0:T(8,128)(2,1)S(1)} %shard_map.74.table_ref), custom_call_target="tpu_custom_call" | custom-call | tf_op jit(solution)/shard_map/pallas_call | solution.py:478
  (16 shorter events, 0.1 us)
Async XLA Ops:
  0.6 3.2 %copy-start.3 = (s32[128,8]{0,1:T(8,128)S(1)}, s32[128,8]{0,1:T(8,128)}, u32[]{:S(2)}) copy-start(s32[128,8]{0,1:T(8,128)} %param.7) | copy-start | bytes 12292
  0.6 3.2 %copy-start.4 = (bf16[128,8]{0,1:T(8,128)(2,1)S(1)}, bf16[128,8]{0,1:T(8,128)(2,1)}, u32[]{:S(2)}) copy-start(bf16[128,8]{0,1:T(8,128)(2,1)} %param.8) | copy-start | bytes 6148
  0.7 3.1 %copy-start.1 = (bf16[128,2048]{1,0:T(8,128)(2,1)S(1)}, bf16[128,2048]{1,0:T(8,128)(2,1)}, u32[]{:S(2)}) copy-start(bf16[128,2048]{1,0:T(8,128)(2,1)} %tokens_ref.1) | copy-start | bytes 1572868
  0.7 3.1 %copy-start.2 = (bf16[128,2048]{1,0:T(8,128)(2,1)S(1)}, bf16[128,2048]{1,0:T(8,128)(2,1)}, u32[]{:S(2)}) copy-start(bf16[128,2048]{1,0:T(8,128)(2,1)} %grads_ref.1) | copy-start | bytes 1572868
  0.7 27.4 %collective-permute-start = (bf16[1,3,512,384]{3,2,1,0:T(8,128)(2,1)}, bf16[1,3,512,384]{3,2,1,0:T(8,128)(2,1)S(1)}, u32[]{:S(2)}, u32[]{:S(2)}) collective-permute-start(bf16[1,3,512,384]{3,2,1,0:T(8,128)(2,1)} %refs_1_.1), channel_id=1, source_target_pairs={{0,8},{8,0},{16,24},{24,16},{1,9},{9,1},{17,25},{25,17},{2,10},{10... | collective-permute-start | bytes 3538952 | tf_op jit(solution)/shard_map/ppermute | solution.py:28
  1.2 29.4 %collective-permute-start.1 = (bf16[1,3,512,384]{3,2,1,0:T(8,128)(2,1)}, bf16[1,3,512,384]{3,2,1,0:T(8,128)(2,1)S(1)}, u32[]{:S(2)}, u32[]{:S(2)}) collective-permute-start(bf16[1,3,512,384]{3,2,1,0:T(8,128)(2,1)} %refs_1_.1), channel_id=1, source_target_pairs={{0,16},{8,24},{16,0},{24,8},{1,17},{9,25},{17,1},{25,9},{2,18},{10... | collective-permute-start | bytes 3538952 | tf_op jit(solution)/shard_map/ppermute | solution.py:28
  3.8 24.3 %copy-start = (bf16[1,3,512,384]{3,2,1,0:T(8,128)(2,1)S(1)}, bf16[1,3,512,384]{3,2,1,0:T(8,128)(2,1)}, u32[]{:S(2)}) copy-start(bf16[1,3,512,384]{3,2,1,0:T(8,128)(2,1)} %refs_1_.1) | copy-start | bytes 3538948
  30.6 2.8 %collective-permute-start.2 = (bf16[1,3,512,384]{3,2,1,0:T(8,128)(2,1)S(1)}, bf16[1,3,512,384]{3,2,1,0:T(8,128)(2,1)S(1)}, u32[]{:S(2)}, u32[]{:S(2)}) collective-permute-start(bf16[1,3,512,384]{3,2,1,0:T(8,128)(2,1)S(1)} %shard_map.71.refs_3_), channel_id=1, source_target_pairs={{0,8},{8,0},{16,24},{24,16},{1,9},{9,1},{17,25},{25,17},{2,10},{10... | collective-permute-start | bytes 3538952 | tf_op jit(solution)/shard_map/ppermute | solution.py:28
  30.6 11.2 %collective-permute-start.3 = (bf16[2,80,512]{2,1,0:T(8,128)(2,1)S(1)}, bf16[2,80,512]{2,1,0:T(8,128)(2,1)S(1)}, u32[]{:S(2)}, u32[]{:S(2)}) collective-permute-start(bf16[2,80,512]{2,1,0:T(8,128)(2,1)S(1)} %get-tuple-element.31), channel_id=1, source_target_pairs={{0,16},{8,24},{16,0},{24,8},{1,17},{9,25},{17,1},{25,9},{2,18},{10... | collective-permute-start | bytes 491528 | tf_op jit(solution)/shard_map/ppermute | solution.py:28
  32.3 9.5 %collective-permute-start.4 = (bf16[2,80,512]{2,1,0:T(8,128)(2,1)S(1)}, bf16[2,80,512]{2,1,0:T(8,128)(2,1)S(1)}, u32[]{:S(2)}, u32[]{:S(2)}) collective-permute-start(bf16[2,80,512]{2,1,0:T(8,128)(2,1)S(1)} %get-tuple-element.32), channel_id=1, source_target_pairs={{0,24},{8,16},{16,8},{24,0},{1,25},{9,17},{17,9},{25,1},{2,26},{10... | collective-permute-start | bytes 491528 | tf_op jit(solution)/shard_map/ppermute | solution.py:28
  35.7 16.6 %all-to-all-start.1 = ((bf16[8,40,512]{2,1,0:T(8,128)(2,1)}), bf16[8,40,512]{2,1,0:T(8,128)(2,1)S(1)}, u32[]{:S(2)}, u32[]{:S(2)}) async-start(bf16[8,40,512]{2,1,0:T(8,128)(2,1)} %get-tuple-element.27), calls=%async_computation.1 | async-start | bytes 655360 | tf_op jit(solution)/shard_map/all_to_all | solution.py:443
  41.8 5.6 %collective-permute-start.8 = (bf16[80,768]{1,0:T(8,128)(2,1)S(1)}, bf16[80,768]{1,0:T(8,128)(2,1)S(1)}, u32[]{:S(2)}, u32[]{:S(2)}) collective-permute-start(bf16[80,768]{1,0:T(8,128)(2,1)S(1)} %get-tuple-element.34.refs_4_), channel_id=1, source_target_pairs={{0,16},{8,24},{16,0},{24,8},{1,17},{9,25},{17,1},{25,9},{2,18},{10... | collective-permute-start | bytes 368648 | tf_op jit(solution)/shard_map/ppermute | solution.py:28
  43.4 6.1 %collective-permute-start.5 = (bf16[2,80,512]{2,1,0:T(8,128)(2,1)S(1)}, bf16[2,80,512]{2,1,0:T(8,128)(2,1)S(1)}, u32[]{:S(2)}, u32[]{:S(2)}) collective-permute-start(bf16[2,80,512]{2,1,0:T(8,128)(2,1)S(1)} %get-tuple-element.33), channel_id=1, source_target_pairs={{0,8},{8,0},{16,24},{24,16},{1,9},{9,1},{17,25},{25,17},{2,10},{10... | collective-permute-start | bytes 491528 | tf_op jit(solution)/shard_map/ppermute | solution.py:28
  43.4 5.4 %collective-permute-start.6 = (bf16[80,768]{1,0:T(8,128)(2,1)S(1)}, bf16[80,768]{1,0:T(8,128)(2,1)S(1)}, u32[]{:S(2)}, u32[]{:S(2)}) collective-permute-start(bf16[80,768]{1,0:T(8,128)(2,1)S(1)} %get-tuple-element.34.refs_4_), channel_id=1, source_target_pairs={{0,8},{8,0},{16,24},{24,16},{1,9},{9,1},{17,25},{25,17},{2,10},{10... | collective-permute-start | bytes 368648 | tf_op jit(solution)/shard_map/ppermute | solution.py:28
  43.9 4.4 %collective-permute-start.9 = (bf16[80,384]{1,0:T(8,128)(2,1)S(1)}, bf16[80,384]{1,0:T(8,128)(2,1)S(1)}, u32[]{:S(2)}, u32[]{:S(2)}) collective-permute-start(bf16[80,384]{1,0:T(8,128)(2,1)S(1)} %get-tuple-element.35.refs_5_), channel_id=1, source_target_pairs={{0,16},{8,24},{16,0},{24,8},{1,17},{9,25},{17,1},{25,9},{2,18},{10... | collective-permute-start | bytes 184328 | tf_op jit(solution)/shard_map/ppermute | solution.py:28
  47.4 2.1 %collective-permute-start.10 = (bf16[80,768]{1,0:T(8,128)(2,1)S(1)}, bf16[80,768]{1,0:T(8,128)(2,1)S(1)}, u32[]{:S(2)}, u32[]{:S(2)}) collective-permute-start(bf16[80,768]{1,0:T(8,128)(2,1)S(1)} %collective-permute-done.8.refs_8_), channel_id=1, source_target_pairs={{0,8},{8,0},{16,24},{24,16},{1,9},{9,1},{17,25},{25,17},{2,10},{10... | collective-permute-start | bytes 368648 | tf_op jit(solution)/shard_map/ppermute | solution.py:28
  47.4 1.4 %collective-permute-start.7 = (bf16[80,384]{1,0:T(8,128)(2,1)S(1)}, bf16[80,384]{1,0:T(8,128)(2,1)S(1)}, u32[]{:S(2)}, u32[]{:S(2)}) collective-permute-start(bf16[80,384]{1,0:T(8,128)(2,1)S(1)} %get-tuple-element.35.refs_5_), channel_id=1, source_target_pairs={{0,8},{8,0},{16,24},{24,16},{1,9},{9,1},{17,25},{25,17},{2,10},{10... | collective-permute-start | bytes 184328 | tf_op jit(solution)/shard_map/ppermute | solution.py:28
  48.3 1.2 %collective-permute-start.11 = (bf16[80,384]{1,0:T(8,128)(2,1)S(1)}, bf16[80,384]{1,0:T(8,128)(2,1)S(1)}, u32[]{:S(2)}, u32[]{:S(2)}) collective-permute-start(bf16[80,384]{1,0:T(8,128)(2,1)S(1)} %collective-permute-done.9.refs_9_), channel_id=1, source_target_pairs={{0,8},{8,0},{16,24},{24,16},{1,9},{9,1},{17,25},{25,17},{2,10},{10... | collective-permute-start | bytes 184328 | tf_op jit(solution)/shard_map/ppermute | solution.py:28

commit v3 on v2

--- a/solution.py
+++ b/solution.py
@@ -479,7 +479,7 @@
         combine_kernel,
         out_specs=anywhere,
         out_shape=shape(token_rows, model_width),
-        scratch_shapes=[pltpu.VMEM((token_rows, model_width), BF16), pltpu.SemaphoreType.DMA((2,))],
+        scratch_shapes=[pltpu.VMEM((token_rows, model_width), BF16), pltpu.SemaphoreType.DMA((4,))],
         compiler_params=params(table, back, tokens),
     )(returned, table)
     return (token_grads, weight_grads)

time: 53.7 us -> 53.7 us (level)
  no operation moved by 1% of the time
where the time goes in v3:
time: 53.7 us; the launch traced here: 53.5 us
  blocking collectives  23.6 us (44%)
  starting transfers between devices  14.2 us (26%)
  Pallas kernels  8.49 us (16%)
  waiting for transfers between devices  6.41 us (12%)
  between operations  0.76 us (1%)
    all_to_all x1, blocking collectives, on_device(): lax.all_to_all(sent, 'expert', split_axis=0, concat_axis=0, tiled=True)  23.6 us
    ppermute x12, starting transfers between devices, swap(): lax.ppermute(value, 'dp', [(i, i ^ bits) for i in range(lax.axis_size('dp...  8.13 us
    all_to_all x1, starting transfers between devices, on_device(): lax.all_to_all(back, 'expert', split_axis=0, concat_axis=0, tiled=True)  6.04 us
    ppermute x12, waiting for transfers between devices, swap(): lax.ppermute(value, 'dp', [(i, i ^ bits) for i in range(lax.axis_size('dp...  5.51 us
    pallas_call x1, Pallas kernels, on_device(): pl.pallas_call(lambda *refs: back_kernel(groups, *refs), out_shape=(shape...  2.3 us
    pallas_call x1, Pallas kernels, on_device(): pl.pallas_call(lambda *refs: grads_kernel(groups, *refs), out_specs=anywh...  1.89 us
    pallas_call x1, Pallas kernels, on_device(): pl.pallas_call(lambda *refs: partial_kernel(groups, *refs), in_specs=[pl....  1.66 us
    pallas_call x1, Pallas kernels, on_device(): pl.pallas_call(combine_kernel, out_specs=anywhere, out_shape=shape(token_...  1.13 us
  transfers between devices with their start and end apart: 13, of which 7 were waited for; matrix products, arithmetic and copies ran while one was open for 0% of the time, Pallas kernels for 14%

profile of v3, /device:TPU:0, one launch (start us, length us, event | category | flops | bytes accessed | tf_op | source)
XLA Modules:
  0.0 53.5 jit_solution(14644155911499119683)
XLA Ops:
  0.7 0.5 collective-permute-start
  1.2 2.6 %collective-permute-start.1 = (bf16[1,3,512,384]{3,2,1,0:T(8,128)(2,1)}, bf16[1,3,512,384]{3,2,1,0:T(8,128)(2,1)S(1)}, u32[]{:S(2)}, u32[]{:S(2)}) collective-permute-start(bf16[1,3,512,384]{3,2,1,0:T(8,128)(2,1)} %refs_1_.1), channel_id=1, source_target_pairs={{0,16},{8,24},{16,0},{24,8},{1,17},{9,25},{17,1},{25,9},{2,18},{10... | collective-permute-start | bytes 3538952 | tf_op jit(solution)/shard_map/ppermute | solution.py:28
  3.8 0.0 copy-start
  3.8 0.6 %shard_map.69 = (bf16[8,80,512]{2,1,0:T(8,128)(2,1)S(1)}, f32[8,128]{1,0:T(8,128)S(1)}) custom-call(s32[8,128]{1,0:T(8,128)S(1)} %bitcast.2, bf16[8,128]{1,0:T(8,128)(2,1)S(1)} %bitcast.3, bf16[128,2048]{1,0:T(8,128)(2,1)S(1)} %copy-done.1, bf16[128,2048]{1,0:T(8,128)(2,1)S(1)} %copy-done.2, f32[8,128]{1,0:T(8,128)S(1)} %shard_map.68._), custom_call_target="tpu_custom_call" | custom-call | tf_op jit(solution)/shard_map/pallas_call | solution.py:376
  4.5 23.6 %all_to_all.10.refs_0_ = bf16[8,80,512]{2,1,0:T(8,128)(2,1)S(1)} all-to-all(bf16[8,80,512]{2,1,0:T(8,128)(2,1)S(1)} %get-tuple-element.19), channel_id=1, replica_groups=mesh['dp'=4,'expert'=8] {'expert'}, dimensions={0} | all-to-all | bytes 1310720 | tf_op jit(solution)/shard_map/all_to_all | solution.py:385
  28.1 1.7 %shard_map.70 = (f32[80,1152]{1,0:T(8,128)S(1)}, bf16[80,2048]{1,0:T(8,128)(2,1)S(1)}, bf16[80,2048]{1,0:T(8,128)(2,1)S(1)}, bf16[2,512,768]{2,1,0:T(8,128)(2,1)...) custom-call(bf16[8,80,512]{2,1,0:T(8,128)(2,1)S(1)} %all_to_all.10.r, ...), custom_call_target="tpu_custom_call" | custom-call | tf_op jit(solution)/shard_map/pallas_call | solution.py:393
  29.7 0.8 %collective-permute-done.1.refs_1_ = bf16[1,3,512,384]{3,2,1,0:T(8,128)(2,1)S(1)} collective-permute-done((bf16[1,3,512,384]{3,2,1,0:T(8,128)(2,1)}, bf16[1,3,512,384]{3,2,1,0:T(8,128)(2,1)S(1)}, u32[]{:S(2)}, u32[]{:S(2)}) %collective-permute-start.1) | collective-permute-done | bytes 1179680 | tf_op jit(solution)/shard_map/ppermute | solution.py:28
  30.6 0.0 collective-permute-start.2
  30.6 1.8 %collective-permute-start.3 = (bf16[2,80,512]{2,1,0:T(8,128)(2,1)S(1)}, bf16[2,80,512]{2,1,0:T(8,128)(2,1)S(1)}, u32[]{:S(2)}, u32[]{:S(2)}) collective-permute-start(bf16[2,80,512]{2,1,0:T(8,128)(2,1)S(1)} %get-tuple-element.31), channel_id=1, source_target_pairs={{0,16},{8,24},{16,0},{24,8},{1,17},{9,25},{17,1},{25,9},{2,18},{10... | collective-permute-start | bytes 491528 | tf_op jit(solution)/shard_map/ppermute | solution.py:28
  32.3 0.1 collective-permute-start.4
  32.5 0.7 %shard_map.72 = (f32[80,1152]{1,0:T(8,128)S(1)}, bf16[1,512,768]{2,1,0:T(8,128)(2,1)S(1)}) custom-call(bf16[80,2048]{1,0:T(8,128)(2,1)S(1)} %get-tuple-element.20.refs_0_, bf16[80,2048]{1,0:T(8,128)(2,1)S(1)} %get-tuple-element.21.refs_1_, f32[80,1152]{1,0:T(8,128)S(1)} %get-tuple-element.22.refs_2_, bf16[1,3,512,384]{3,2,1,0:T(8,128)(2,1)S(1)} %shard_map.71.refs_3_), custom_call_target="tpu_custom_call" | custom-call | tf_op jit(solution)/shard_map/pallas_call | solution.py:425
  33.1 0.3 collective-permute-done.2.refs_5_
  33.4 2.3 %shard_map.73 = (bf16[80,1152]{1,0:T(8,128)(2,1)S(1)}, bf16[8,40,512]{2,1,0:T(8,128)(2,1)}) custom-call(bf16[80,2048]{1,0:T(8,128)(2,1)S(1)} %get-tuple-element.20.refs_0_, bf16[80,2048]{1,0:T(8,128)(2,1)S(1)} %get-tuple-element.21.refs_1_, f32[80,1152]{1,0:T(8,128)S(1)} %get-tuple-element.24.refs_2_, bf16[2,512,768]{2,1,0:T(8,128)(2,1)S(1)} %get-tuple-element.25.refs_3_, ...), custom_call_target="tpu_custom_call" | custom-call | flops 1000000 | bytes 100000 | tf_op jit(solution)/shard_map/pallas_call | solution.py:436
  35.7 6.0 %all-to-all-start.1 = ((bf16[8,40,512]{2,1,0:T(8,128)(2,1)}), bf16[8,40,512]{2,1,0:T(8,128)(2,1)S(1)}, u32[]{:S(2)}, u32[]{:S(2)}) async-start(bf16[8,40,512]{2,1,0:T(8,128)(2,1)} %get-tuple-element.27), calls=%async_computation.1 | async-start | bytes 655360 | tf_op jit(solution)/shard_map/all_to_all | solution.py:443
  41.8 0.0 collective-permute-done.3.refs_1_.refs_2_
  41.8 0.0 collective-permute-done.4.refs_2_.refs_3_
  41.8 1.6 %collective-permute-start.8 = (bf16[80,768]{1,0:T(8,128)(2,1)S(1)}, bf16[80,768]{1,0:T(8,128)(2,1)S(1)}, u32[]{:S(2)}, u32[]{:S(2)}) collective-permute-start(bf16[80,768]{1,0:T(8,128)(2,1)S(1)} %get-tuple-element.34.refs_4_), channel_id=1, source_target_pairs={{0,16},{8,24},{16,0},{24,8},{1,17},{9,25},{17,1},{25,9},{2,18},{10... | collective-permute-start | bytes 368648 | tf_op jit(solution)/shard_map/ppermute | solution.py:28
  43.4 0.0 collective-permute-start.5
  43.4 0.5 collective-permute-start.6
  43.9 0.5 collective-permute-start.9
  44.4 3.0 %collective-permute-done.8.refs_8_ = bf16[80,768]{1,0:T(8,128)(2,1)S(1)} collective-permute-done((bf16[80,768]{1,0:T(8,128)(2,1)S(1)}, bf16[80,768]{1,0:T(8,128)(2,1)S(1)}, u32[]{:S(2)}, u32[]{:S(2)}) %collective-permute-start.8) | collective-permute-done | bytes 122912 | tf_op jit(solution)/shard_map/ppermute | solution.py:28
  47.4 0.5 collective-permute-start.7
  47.9 0.4 collective-permute-done.9.refs_9_
  48.3 0.2 shard_map.74.table_ref
  48.5 0.4 collective-permute-done.7.refs_7_
  48.8 0.0 collective-permute-done.6.refs_6_
  48.8 0.7 %collective-permute-done.11.refs_11_ = bf16[80,384]{1,0:T(8,128)(2,1)S(1)} collective-permute-done((bf16[80,384]{1,0:T(8,128)(2,1)S(1)}, bf16[80,384]{1,0:T(8,128)(2,1)S(1)}, u32[]{:S(2)}, u32[]{:S(2)}) %collective-permute-start.11) | collective-permute-done | bytes 61472 | tf_op jit(solution)/shard_map/ppermute | solution.py:28
  49.5 0.0 collective-permute-done.5.refs_1_
  49.5 0.0 collective-permute-done.10.refs_10_
  49.5 1.9 %shard_map.78 = f32[1,3,512,384]{3,2,1,0:T(8,128)} custom-call(bf16[4,80,512]{2,1,0:T(8,128)(2,1)S(1)} %get-tuple-element.29.local_ref.refs_0_, bf16[2,80,512]{2,1,0:T(8,128)(2,1)S(1)} %collective-permute-done.5.refs_1_, bf16[2,80,512]{2,1,0:T(8,128)(2,1)S(1)} %collective-permute-done.3.refs_1_.refs_2_, ...), custom_call_target="tpu_custom_call" | custom-call | flops 377487360 | bytes 2359296 | tf_op jit(solution)/shard_map/pallas_call | solution.py:466
  51.4 0.9 %all-to-all-done.1.returned_ref = bf16[8,40,512]{2,1,0:T(8,128)(2,1)S(1)} async-done(((bf16[8,40,512]{2,1,0:T(8,128)(2,1)}), bf16[8,40,512]{2,1,0:T(8,128)(2,1)S(1)}, u32[]{:S(2)}, u32[]{:S(2)}) %all-to-all-start.1) | async-done | bytes 327712 | tf_op jit(solution)/shard_map/all_to_all | solution.py:443
  52.3 1.1 %shard_map.75 = bf16[128,2048]{1,0:T(8,128)(2,1)} custom-call(bf16[8,40,512]{2,1,0:T(8,128)(2,1)S(1)} %all-to-all-done.1.returned_ref, bf16[512,320]{1,0:T(8,128)(2,1)S(1)} %shard_map.74.table_ref), custom_call_target="tpu_custom_call" | custom-call | tf_op jit(solution)/shard_map/pallas_call | solution.py:478
  (16 shorter events, 0.1 us)
Async XLA Ops:
  0.6 3.2 %copy-start.3 = (s32[128,8]{0,1:T(8,128)S(1)}, s32[128,8]{0,1:T(8,128)}, u32[]{:S(2)}) copy-start(s32[128,8]{0,1:T(8,128)} %param.7) | copy-start | bytes 12292
  0.6 3.2 %copy-start.4 = (bf16[128,8]{0,1:T(8,128)(2,1)S(1)}, bf16[128,8]{0,1:T(8,128)(2,1)}, u32[]{:S(2)}) copy-start(bf16[128,8]{0,1:T(8,128)(2,1)} %param.8) | copy-start | bytes 6148
  0.7 3.1 %copy-start.1 = (bf16[128,2048]{1,0:T(8,128)(2,1)S(1)}, bf16[128,2048]{1,0:T(8,128)(2,1)}, u32[]{:S(2)}) copy-start(bf16[128,2048]{1,0:T(8,128)(2,1)} %tokens_ref.1) | copy-start | bytes 1572868
  0.7 3.1 %copy-start.2 = (bf16[128,2048]{1,0:T(8,128)(2,1)S(1)}, bf16[128,2048]{1,0:T(8,128)(2,1)}, u32[]{:S(2)}) copy-start(bf16[128,2048]{1,0:T(8,128)(2,1)} %grads_ref.1) | copy-start | bytes 1572868
  0.7 27.4 %collective-permute-start = (bf16[1,3,512,384]{3,2,1,0:T(8,128)(2,1)}, bf16[1,3,512,384]{3,2,1,0:T(8,128)(2,1)S(1)}, u32[]{:S(2)}, u32[]{:S(2)}) collective-permute-start(bf16[1,3,512,384]{3,2,1,0:T(8,128)(2,1)} %refs_1_.1), channel_id=1, source_target_pairs={{0,8},{8,0},{16,24},{24,16},{1,9},{9,1},{17,25},{25,17},{2,10},{10... | collective-permute-start | bytes 3538952 | tf_op jit(solution)/shard_map/ppermute | solution.py:28
  1.2 29.4 %collective-permute-start.1 = (bf16[1,3,512,384]{3,2,1,0:T(8,128)(2,1)}, bf16[1,3,512,384]{3,2,1,0:T(8,128)(2,1)S(1)}, u32[]{:S(2)}, u32[]{:S(2)}) collective-permute-start(bf16[1,3,512,384]{3,2,1,0:T(8,128)(2,1)} %refs_1_.1), channel_id=1, source_target_pairs={{0,16},{8,24},{16,0},{24,8},{1,17},{9,25},{17,1},{25,9},{2,18},{10... | collective-permute-start | bytes 3538952 | tf_op jit(solution)/shard_map/ppermute | solution.py:28
  3.8 24.3 %copy-start = (bf16[1,3,512,384]{3,2,1,0:T(8,128)(2,1)S(1)}, bf16[1,3,512,384]{3,2,1,0:T(8,128)(2,1)}, u32[]{:S(2)}) copy-start(bf16[1,3,512,384]{3,2,1,0:T(8,128)(2,1)} %refs_1_.1) | copy-start | bytes 3538948
  30.6 2.8 %collective-permute-start.2 = (bf16[1,3,512,384]{3,2,1,0:T(8,128)(2,1)S(1)}, bf16[1,3,512,384]{3,2,1,0:T(8,128)(2,1)S(1)}, u32[]{:S(2)}, u32[]{:S(2)}) collective-permute-start(bf16[1,3,512,384]{3,2,1,0:T(8,128)(2,1)S(1)} %shard_map.71.refs_3_), channel_id=1, source_target_pairs={{0,8},{8,0},{16,24},{24,16},{1,9},{9,1},{17,25},{25,17},{2,10},{10... | collective-permute-start | bytes 3538952 | tf_op jit(solution)/shard_map/ppermute | solution.py:28
  30.6 11.2 %collective-permute-start.3 = (bf16[2,80,512]{2,1,0:T(8,128)(2,1)S(1)}, bf16[2,80,512]{2,1,0:T(8,128)(2,1)S(1)}, u32[]{:S(2)}, u32[]{:S(2)}) collective-permute-start(bf16[2,80,512]{2,1,0:T(8,128)(2,1)S(1)} %get-tuple-element.31), channel_id=1, source_target_pairs={{0,16},{8,24},{16,0},{24,8},{1,17},{9,25},{17,1},{25,9},{2,18},{10... | collective-permute-start | bytes 491528 | tf_op jit(solution)/shard_map/ppermute | solution.py:28
  32.3 9.5 %collective-permute-start.4 = (bf16[2,80,512]{2,1,0:T(8,128)(2,1)S(1)}, bf16[2,80,512]{2,1,0:T(8,128)(2,1)S(1)}, u32[]{:S(2)}, u32[]{:S(2)}) collective-permute-start(bf16[2,80,512]{2,1,0:T(8,128)(2,1)S(1)} %get-tuple-element.32), channel_id=1, source_target_pairs={{0,24},{8,16},{16,8},{24,0},{1,25},{9,17},{17,9},{25,1},{2,26},{10... | collective-permute-start | bytes 491528 | tf_op jit(solution)/shard_map/ppermute | solution.py:28
  35.7 16.6 %all-to-all-start.1 = ((bf16[8,40,512]{2,1,0:T(8,128)(2,1)}), bf16[8,40,512]{2,1,0:T(8,128)(2,1)S(1)}, u32[]{:S(2)}, u32[]{:S(2)}) async-start(bf16[8,40,512]{2,1,0:T(8,128)(2,1)} %get-tuple-element.27), calls=%async_computation.1 | async-start | bytes 655360 | tf_op jit(solution)/shard_map/all_to_all | solution.py:443
  41.8 5.6 %collective-permute-start.8 = (bf16[80,768]{1,0:T(8,128)(2,1)S(1)}, bf16[80,768]{1,0:T(8,128)(2,1)S(1)}, u32[]{:S(2)}, u32[]{:S(2)}) collective-permute-start(bf16[80,768]{1,0:T(8,128)(2,1)S(1)} %get-tuple-element.34.refs_4_), channel_id=1, source_target_pairs={{0,16},{8,24},{16,0},{24,8},{1,17},{9,25},{17,1},{25,9},{2,18},{10... | collective-permute-start | bytes 368648 | tf_op jit(solution)/shard_map/ppermute | solution.py:28
  43.4 6.1 %collective-permute-start.5 = (bf16[2,80,512]{2,1,0:T(8,128)(2,1)S(1)}, bf16[2,80,512]{2,1,0:T(8,128)(2,1)S(1)}, u32[]{:S(2)}, u32[]{:S(2)}) collective-permute-start(bf16[2,80,512]{2,1,0:T(8,128)(2,1)S(1)} %get-tuple-element.33), channel_id=1, source_target_pairs={{0,8},{8,0},{16,24},{24,16},{1,9},{9,1},{17,25},{25,17},{2,10},{10... | collective-permute-start | bytes 491528 | tf_op jit(solution)/shard_map/ppermute | solution.py:28
  43.4 5.4 %collective-permute-start.6 = (bf16[80,768]{1,0:T(8,128)(2,1)S(1)}, bf16[80,768]{1,0:T(8,128)(2,1)S(1)}, u32[]{:S(2)}, u32[]{:S(2)}) collective-permute-start(bf16[80,768]{1,0:T(8,128)(2,1)S(1)} %get-tuple-element.34.refs_4_), channel_id=1, source_target_pairs={{0,8},{8,0},{16,24},{24,16},{1,9},{9,1},{17,25},{25,17},{2,10},{10... | collective-permute-start | bytes 368648 | tf_op jit(solution)/shard_map/ppermute | solution.py:28
  43.9 4.4 %collective-permute-start.9 = (bf16[80,384]{1,0:T(8,128)(2,1)S(1)}, bf16[80,384]{1,0:T(8,128)(2,1)S(1)}, u32[]{:S(2)}, u32[]{:S(2)}) collective-permute-start(bf16[80,384]{1,0:T(8,128)(2,1)S(1)} %get-tuple-element.35.refs_5_), channel_id=1, source_target_pairs={{0,16},{8,24},{16,0},{24,8},{1,17},{9,25},{17,1},{25,9},{2,18},{10... | collective-permute-start | bytes 184328 | tf_op jit(solution)/shard_map/ppermute | solution.py:28
  47.4 2.1 %collective-permute-start.10 = (bf16[80,768]{1,0:T(8,128)(2,1)S(1)}, bf16[80,768]{1,0:T(8,128)(2,1)S(1)}, u32[]{:S(2)}, u32[]{:S(2)}) collective-permute-start(bf16[80,768]{1,0:T(8,128)(2,1)S(1)} %collective-permute-done.8.refs_8_), channel_id=1, source_target_pairs={{0,8},{8,0},{16,24},{24,16},{1,9},{9,1},{17,25},{25,17},{2,10},{10... | collective-permute-start | bytes 368648 | tf_op jit(solution)/shard_map/ppermute | solution.py:28
  47.4 1.4 %collective-permute-start.7 = (bf16[80,384]{1,0:T(8,128)(2,1)S(1)}, bf16[80,384]{1,0:T(8,128)(2,1)S(1)}, u32[]{:S(2)}, u32[]{:S(2)}) collective-permute-start(bf16[80,384]{1,0:T(8,128)(2,1)S(1)} %get-tuple-element.35.refs_5_), channel_id=1, source_target_pairs={{0,8},{8,0},{16,24},{24,16},{1,9},{9,1},{17,25},{25,17},{2,10},{10... | collective-permute-start | bytes 184328 | tf_op jit(solution)/shard_map/ppermute | solution.py:28
  48.3 1.2 %collective-permute-start.11 = (bf16[80,384]{1,0:T(8,128)(2,1)S(1)}, bf16[80,384]{1,0:T(8,128)(2,1)S(1)}, u32[]{:S(2)}, u32[]{:S(2)}) collective-permute-start(bf16[80,384]{1,0:T(8,128)(2,1)S(1)} %collective-permute-done.9.refs_9_), channel_id=1, source_target_pairs={{0,8},{8,0},{16,24},{24,16},{1,9},{9,1},{17,25},{25,17},{2,10},{10... | collective-permute-start | bytes 184328 | tf_op jit(solution)/shard_map/ppermute | solution.py:28
